TPU v7x, 512 devices: a whole 4x4x16 slice. The times are simulated.
512 devices in a mesh: dp: 16 (over y, x), seq: 32 (over z, core).
Axes of the slice: x: 4, y: 4, z: 16, core: 2. Of those that a mesh axis runs over, the one named last changes fastest.
Arguments:
- tokens: bfloat16 [4096, 4096], P('seq'), may hold values from -6 to 6
- w_in: bfloat16 [4096, 20608], P('seq', 'dp'), may hold values from -0.09375 to 0.09375
- conv_weight: float32 [4, 12288], P(None, 'dp'), may hold values from -0.8 to 0.8
- conv_bias: float32 [12288], P('dp'), may hold values from -0.5 to 0.5
- dt_bias: float32 [128], P('dp'), may hold values from -2 to 1
- decay_rate: float32 [128], P('dp'), may hold values from 1e-06 to 0.3
- skip_gain: float32 [128], P('dp'), may hold values from 0.5 to 1.5
- norm_gain: float32 [8192], P('dp'), may hold values from 0.5 to 1.5
- w_out: bfloat16 [8192, 4096], P('dp', 'seq'), may hold values from -0.0625 to 0.0625
Outputs:
- mixed: bfloat16 [4096, 4096], P('seq', 'dp')
All inputs are finite; a program needn't handle non-finite values.
Results may differ from a plain program's by a relative error of at most 0.025.
Values may be sent and summed in bfloat16 or wider, within the bound.
A program may use at most 64 MiB of HBM per device.

v0:
```python
import jax
import jax.numpy as jnp
from jax import lax
from jax.sharding import PartitionSpec as P

P_SIZE = 64
N = 128
KCONV = 4
BLOCK = 128
HG = 8
XG = 768
CG = 1288


def from_behind(block, axis, distance):
    devices = range(lax.axis_size(axis))
    route = [(i - distance, i) for i in devices if i - distance in devices]
    return lax.ppermute(block, axis, route)


def combine(earlier, later):
    return (earlier[0] * later[0], later[0][:, :, None, None] * earlier[1] + later[1])


def per_device(
    tokens, w_in, conv_weight, conv_bias, dt_bias, decay_rate, skip_gain, norm_gain, w_out
):
    rows = tokens.shape[0]
    heads_dev = decay_rate.shape[0]
    groups_dev = heads_dev // HG
    blocks = rows // BLOCK
    proj = jnp.dot(
        tokens, lax.all_gather(w_in, "seq", axis=0, tiled=True), preferred_element_type=jnp.float32
    )
    proj = proj.astype(jnp.bfloat16).reshape(rows, groups_dev, CG)
    xbc = proj[:, :, HG * P_SIZE : HG * P_SIZE + XG]
    rim = from_behind(xbc[rows - (KCONV - 1) :], "seq", 1)
    padded = jnp.concatenate([rim, xbc], axis=0).astype(jnp.float32)
    taps = conv_weight.reshape(KCONV, groups_dev, XG)
    conv = jnp.zeros((rows, groups_dev, XG), jnp.float32) + conv_bias.reshape(groups_dev, XG)
    for k in range(KCONV):
        conv = conv + taps[k] * padded[k : k + rows]
    act = jax.nn.silu(conv)
    xs = act[:, :, : HG * P_SIZE].reshape(blocks, BLOCK, groups_dev, HG, P_SIZE)
    bmat = act[:, :, HG * P_SIZE : HG * P_SIZE + N].reshape(blocks, BLOCK, groups_dev, N)
    cmat = act[:, :, HG * P_SIZE + N :].reshape(blocks, BLOCK, groups_dev, N)
    draw = proj[:, :, HG * P_SIZE + XG :].astype(jnp.float32).reshape(rows, heads_dev)
    dt = jax.nn.softplus(draw + dt_bias)
    logdec = (-dt * decay_rate).reshape(blocks, BLOCK, groups_dev, HG)
    dtq = dt.reshape(blocks, BLOCK, groups_dev, HG)
    cum = jnp.cumsum(logdec, axis=1)
    scores = jnp.einsum("btgn,bsgn->btsg", cmat, bmat, precision=lax.Precision.HIGHEST)
    later = lax.broadcasted_iota(jnp.int32, (BLOCK, BLOCK), 0) >= lax.broadcasted_iota(
        jnp.int32, (BLOCK, BLOCK), 1
    )
    later = later[None, :, :, None, None]
    gap = cum[:, :, None] - cum[:, None, :]
    weights = jnp.where(later, jnp.exp(jnp.where(later, gap, 0.0)), 0.0)
    mixing = scores[..., None] * weights * dtq[:, None]
    ydiag = jnp.einsum("btsgh,bsghp->btghp", mixing, xs, precision=lax.Precision.HIGHEST)
    tail = jnp.exp(cum[:, -1:] - cum) * dtq
    block_state = jnp.einsum(
        "bsgh,bsgn,bsghp->bghnp", tail, bmat, xs, precision=lax.Precision.HIGHEST
    )
    block_decay = jnp.exp(cum[:, -1])

    def gather_blocks(carry, item):
        return (combine(carry, item), carry)

    unit = (
        jnp.ones((groups_dev, HG), jnp.float32),
        jnp.zeros((groups_dev, HG, N, P_SIZE), jnp.float32),
    )
    (dev_decay, dev_state), (pre_decay, pre_state) = lax.scan(
        gather_blocks, unit, (block_decay, block_state)
    )

    def relay(step, incoming):
        outgoing = dev_decay[:, :, None, None] * incoming + dev_state
        return from_behind(outgoing.astype(jnp.bfloat16), "seq", 1).astype(outgoing.dtype)

    incoming = lax.fori_loop(
        0, lax.axis_size("seq") - 1, relay, jnp.zeros((groups_dev, HG, N, P_SIZE), jnp.float32)
    )
    block_in = pre_decay[:, :, :, None, None] * incoming[None] + pre_state
    yoff = jnp.einsum("btgn,bghnp->btghp", cmat, block_in, precision=lax.Precision.HIGHEST)
    yoff = yoff * jnp.exp(cum)[..., None]
    ys = ydiag + yoff + skip_gain.reshape(groups_dev, HG)[None, None, :, :, None] * xs
    zpart = proj[:, :, : HG * P_SIZE].astype(jnp.float32)
    gated = ys.reshape(rows, groups_dev, HG * P_SIZE) * jax.nn.silu(zpart)
    meansq = jnp.mean(gated * gated, axis=2, keepdims=True)
    normed = gated * lax.rsqrt(meansq + 1e-05) * norm_gain.reshape(groups_dev, HG * P_SIZE)
    normed = normed.reshape(rows, heads_dev * P_SIZE).astype(jnp.bfloat16)
    terms = jnp.dot(
        normed, lax.all_gather(w_out, "seq", axis=1, tiled=True), preferred_element_type=jnp.float32
    )
    return lax.psum_scatter(terms.astype(jnp.bfloat16), "dp", scatter_dimension=1, tiled=True)


def solution(mesh):
    placed = (
        P("seq", None),
        P("seq", "dp"),
        P(None, "dp"),
        P("dp"),
        P("dp"),
        P("dp"),
        P("dp"),
        P("dp"),
        P("dp", "seq"),
    )
    return jax.shard_map(
        per_device, mesh=mesh, in_specs=placed, out_specs=P("seq", "dp"), check_vma=False
    )
```

profile of v0, /device:TPU:1, one launch (start us, length us, event | category | flops | bytes accessed | tf_op | source)
XLA Modules:
  0.0 521.8 jit_solution(3478152572014117301)
XLA Ops:
  9.0 109.8 %all-gather.3.cloned.1.call-done = bf16[4096,1288]{0,1:T(8,128)(2,1)} async-done(((bf16[128,1288]{0,1:T(8,128)(2,1)}), bf16[4096,1288]{0,1:T(8,128)(2,1)}) %all-gather.3.cloned.1.call-update) | async-done | bytes 10551312 | tf_op jit(solution)/shard_map/all_gather | solution.py:33
  118.8 5.7 %fusion.2 = bf16[128,1,1288]{0,2,1:T(8,128)(2,1)S(1)} fusion(bf16[128,4096]{1,0:T(8,128)(2,1)S(1)} %copy-done, bf16[4096,1288]{0,1:T(8,128)(2,1)} %all-gather.3.cloned.1.call-done), kind=kOutput, calls=%fused_computation.5 | convolution fusion | flops 1350730752 | bytes 11929600 | tf_op jit(solution)/shard_map/dot_general | solution.py:32
  125.0 5.8 %collective-permute-start.1 = (bf16[3,1,768]{0,2,1:T(8,128)(2,1)S(1)}, bf16[3,1,768]{0,2,1:T(8,128)(2,1)S(1)}, u32[]{:S(2)}, u32[]{:S(2)}) collective-permute-start(bf16[3,1,768]{0,2,1:T(8,128)(2,1)S(1)} %slice.70), channel_id=1, source_target_pairs={{0,1},{1,2},{2,3},{3,4},{4,5},{5,6},{6,7},{7,8},{8,9},{9,10},{10,1... | collective-permute-start | bytes 13832 | tf_op jit(solution)/shard_map/ppermute | solution.py:18
  135.9 264.7 %while.3 = (s32[]{:T(128)}, f32[1,8,128,64]{3,2,1,0:T(8,128)S(1)}, f32[1,8]{1,0:T(1,128)S(1)}, f32[1,8,128,64]{3,2,1,0:T(8,128)S(1)}, s32[]{:T(128)}, /*index=5*/s32[]{:T(128)}) while((s32[]{:T(128)}, f32[1,8,128,64]{3,2,1,0:T(8,128)S(1)}, f32[1,8]{1,0:T(1,128)S(1)}, f32[1,8,128,64]{3,2,1,0:T(8,128)S(1)}, s32[]{:T(128)}, ...), condition=%wide.region_2.3_spmd.clone, body=%wide.region_1.2_spmd.clone.sunk | while | flops 327683 | bytes 1573015 | solution.py:82
  136.1 4.4 collective-permute-start
  140.5 4.7 collective-permute-done
  145.4 4.4 collective-permute-start
  149.8 4.9 collective-permute-done
  154.9 4.4 collective-permute-start
  159.3 4.7 collective-permute-done
  164.2 4.4 collective-permute-start
  168.6 4.6 collective-permute-done
  173.4 4.4 collective-permute-start
  177.8 5.0 collective-permute-done
  182.9 4.4 collective-permute-start
  187.3 4.9 collective-permute-done
  192.5 4.4 collective-permute-start
  196.9 4.0 collective-permute-done
  201.0 4.4 collective-permute-start
  208.9 4.4 collective-permute-start
  213.3 3.3 collective-permute-done
  216.8 4.4 collective-permute-start
  221.2 3.3 collective-permute-done
  224.7 4.4 collective-permute-start
  229.1 3.3 collective-permute-done
  232.6 4.4 collective-permute-start
  237.0 3.3 collective-permute-done
  240.5 4.4 collective-permute-start
  248.4 4.4 collective-permute-start
  256.3 4.4 collective-permute-start
  264.1 4.4 collective-permute-start
  272.0 4.4 collective-permute-start
  279.9 4.4 collective-permute-start
  287.8 4.4 collective-permute-start
  295.7 4.4 collective-permute-start
  303.6 4.4 collective-permute-start
  311.5 4.4 collective-permute-start
  319.3 5.2 collective-permute-start
  328.0 5.6 %collective-permute-start = (bf16[1,8,128,64]{3,2,1,0:T(8,128)(2,1)S(1)}, bf16[1,8,128,64]{3,2,1,0:T(8,128)(2,1)S(1)}, u32[]{:S(2)}, u32[]{:S(2)}) collective-permute-start(bf16[1,8,128,64]{3,2,1,0:T(8,128)(2,1)S(1)} %fusion.67), channel_id=1, source_target_pairs={{0,1},{1,2},{2,3},{3,4},{4,5},{5,6},{6,7},{7,8},{8,9},{9,10},{10,1... | collective-permute-start | bytes 393224 | tf_op jit(solution)/shard_map/while/body/eval_jaxpr/ppermute | solution.py:18
  337.1 5.6 %collective-permute-start = (bf16[1,8,128,64]{3,2,1,0:T(8,128)(2,1)S(1)}, bf16[1,8,128,64]{3,2,1,0:T(8,128)(2,1)S(1)}, u32[]{:S(2)}, u32[]{:S(2)}) collective-permute-start(bf16[1,8,128,64]{3,2,1,0:T(8,128)(2,1)S(1)} %fusion.67), channel_id=1, source_target_pairs={{0,1},{1,2},{2,3},{3,4},{4,5},{5,6},{6,7},{7,8},{8,9},{9,10},{10,1... | collective-permute-start | bytes 393224 | tf_op jit(solution)/shard_map/while/body/eval_jaxpr/ppermute | solution.py:18
  346.2 5.6 %collective-permute-start = (bf16[1,8,128,64]{3,2,1,0:T(8,128)(2,1)S(1)}, bf16[1,8,128,64]{3,2,1,0:T(8,128)(2,1)S(1)}, u32[]{:S(2)}, u32[]{:S(2)}) collective-permute-start(bf16[1,8,128,64]{3,2,1,0:T(8,128)(2,1)S(1)} %fusion.67), channel_id=1, source_target_pairs={{0,1},{1,2},{2,3},{3,4},{4,5},{5,6},{6,7},{7,8},{8,9},{9,10},{10,1... | collective-permute-start | bytes 393224 | tf_op jit(solution)/shard_map/while/body/eval_jaxpr/ppermute | solution.py:18
  355.3 5.6 %collective-permute-start = (bf16[1,8,128,64]{3,2,1,0:T(8,128)(2,1)S(1)}, bf16[1,8,128,64]{3,2,1,0:T(8,128)(2,1)S(1)}, u32[]{:S(2)}, u32[]{:S(2)}) collective-permute-start(bf16[1,8,128,64]{3,2,1,0:T(8,128)(2,1)S(1)} %fusion.67), channel_id=1, source_target_pairs={{0,1},{1,2},{2,3},{3,4},{4,5},{5,6},{6,7},{7,8},{8,9},{9,10},{10,1... | collective-permute-start | bytes 393224 | tf_op jit(solution)/shard_map/while/body/eval_jaxpr/ppermute | solution.py:18
  364.4 5.6 %collective-permute-start = (bf16[1,8,128,64]{3,2,1,0:T(8,128)(2,1)S(1)}, bf16[1,8,128,64]{3,2,1,0:T(8,128)(2,1)S(1)}, u32[]{:S(2)}, u32[]{:S(2)}) collective-permute-start(bf16[1,8,128,64]{3,2,1,0:T(8,128)(2,1)S(1)} %fusion.67), channel_id=1, source_target_pairs={{0,1},{1,2},{2,3},{3,4},{4,5},{5,6},{6,7},{7,8},{8,9},{9,10},{10,1... | collective-permute-start | bytes 393224 | tf_op jit(solution)/shard_map/while/body/eval_jaxpr/ppermute | solution.py:18
  373.5 5.6 %collective-permute-start = (bf16[1,8,128,64]{3,2,1,0:T(8,128)(2,1)S(1)}, bf16[1,8,128,64]{3,2,1,0:T(8,128)(2,1)S(1)}, u32[]{:S(2)}, u32[]{:S(2)}) collective-permute-start(bf16[1,8,128,64]{3,2,1,0:T(8,128)(2,1)S(1)} %fusion.67), channel_id=1, source_target_pairs={{0,1},{1,2},{2,3},{3,4},{4,5},{5,6},{6,7},{7,8},{8,9},{9,10},{10,1... | collective-permute-start | bytes 393224 | tf_op jit(solution)/shard_map/while/body/eval_jaxpr/ppermute | solution.py:18
  382.6 5.6 %collective-permute-start = (bf16[1,8,128,64]{3,2,1,0:T(8,128)(2,1)S(1)}, bf16[1,8,128,64]{3,2,1,0:T(8,128)(2,1)S(1)}, u32[]{:S(2)}, u32[]{:S(2)}) collective-permute-start(bf16[1,8,128,64]{3,2,1,0:T(8,128)(2,1)S(1)} %fusion.67), channel_id=1, source_target_pairs={{0,1},{1,2},{2,3},{3,4},{4,5},{5,6},{6,7},{7,8},{8,9},{9,10},{10,1... | collective-permute-start | bytes 393224 | tf_op jit(solution)/shard_map/while/body/eval_jaxpr/ppermute | solution.py:18
  391.7 5.6 %collective-permute-start = (bf16[1,8,128,64]{3,2,1,0:T(8,128)(2,1)S(1)}, bf16[1,8,128,64]{3,2,1,0:T(8,128)(2,1)S(1)}, u32[]{:S(2)}, u32[]{:S(2)}) collective-permute-start(bf16[1,8,128,64]{3,2,1,0:T(8,128)(2,1)S(1)} %fusion.67), channel_id=1, source_target_pairs={{0,1},{1,2},{2,3},{3,4},{4,5},{5,6},{6,7},{7,8},{8,9},{9,10},{10,1... | collective-permute-start | bytes 393224 | tf_op jit(solution)/shard_map/while/body/eval_jaxpr/ppermute | solution.py:18
  404.0 4.0 convolution_convert_fusion
  408.1 107.2 %reduce-scatter.2.cloned.1.call-done = bf16[128,256]{1,0:T(8,128)(2,1)} async-done(((bf16[128,4096]{1,0:T(8,128)(2,1)}), bf16[128,256]{1,0:T(8,128)(2,1)}) %reduce-scatter.2.cloned.1.call-update) | async-done | bytes 65552 | tf_op jit(solution)/shard_map/reduce_scatter | solution.py:97
  (127 shorter events, 82.4 us)
Async XLA Ops:
  6.5 112.3 %copy-start = (bf16[128,4096]{1,0:T(8,128)(2,1)S(1)}, bf16[128,4096]{1,0:T(8,128)(2,1)}, u32[]{:S(2)}) copy-start(bf16[128,4096]{1,0:T(8,128)(2,1)} %param.11) | copy-start | bytes 3145732
  6.5 112.3 %all-gather.3.cloned.1.call-start = ((), (), s32[]{:S(2)}) async-start(), calls=%async_computation.1 | async-start | bytes 10881024 | tf_op jit(solution)/shard_map/all_gather | solution.py:33
  7.3 396.8 %all-gather.5.cloned.1.call-start = ((), (), s32[]{:S(2)}) async-start(), calls=%async_computation.2 | async-start | bytes 4325376 | tf_op jit(solution)/shard_map/all_gather | solution.py:95
  8.0 507.2 %reduce-scatter.2.cloned.1.call-start = ((), (), s32[]{:S(2)}) async-start(), calls=%async_computation.3 | async-start | bytes 1114112 | tf_op jit(solution)/shard_map/reduce_scatter | solution.py:97
  9.0 115.6 %copy-start.4 = (f32[8]{0:T(128)S(1)}, f32[8]{0:T(128)}, u32[]{:S(2)}) copy-start(f32[8]{0:T(128)} %param.15) | copy-start | bytes 100
  9.0 115.6 %copy-start.5 = (f32[8]{0:T(128)S(1)}, f32[8]{0:T(128)}, u32[]{:S(2)}) copy-start(f32[8]{0:T(128)} %param.16) | copy-start | bytes 100
  9.0 124.6 %copy-start.2 = (f32[768]{0:T(1024)S(1)}, f32[768]{0:T(1024)}, u32[]{:S(2)}) copy-start(f32[768]{0:T(1024)} %param.14) | copy-start | bytes 9220
  125.0 8.4 %collective-permute-start.1 = (bf16[3,1,768]{0,2,1:T(8,128)(2,1)S(1)}, bf16[3,1,768]{0,2,1:T(8,128)(2,1)S(1)}, u32[]{:S(2)}, u32[]{:S(2)}) collective-permute-start(bf16[3,1,768]{0,2,1:T(8,128)(2,1)S(1)} %slice.70), channel_id=1, source_target_pairs={{0,1},{1,2},{2,3},{3,4},{4,5},{5,6},{6,7},{7,8},{8,9},{9,10},{10,1... | collective-permute-start | bytes 13832 | tf_op jit(solution)/shard_map/ppermute | solution.py:18
  134.5 0.7 copy-start.1
  135.9 265.7 %copy-start.6 = (f32[8]{0:T(128)S(1)}, f32[8]{0:T(128)}, u32[]{:S(2)}) copy-start(f32[8]{0:T(128)} %param.17) | copy-start | bytes 100
  135.9 268.1 %copy-start.3 = (f32[512]{0:T(512)S(1)}, f32[512]{0:T(512)}, u32[]{:S(2)}) copy-start(f32[512]{0:T(512)} %param.18) | copy-start | bytes 6148
  136.1 9.1 %collective-permute-start = (bf16[1,8,128,64]{3,2,1,0:T(8,128)(2,1)S(1)}, bf16[1,8,128,64]{3,2,1,0:T(8,128)(2,1)S(1)}, u32[]{:S(2)}, u32[]{:S(2)}) collective-permute-start(bf16[1,8,128,64]{3,2,1,0:T(8,128)(2,1)S(1)} %fusion.67), channel_id=1, source_target_pairs={{0,1},{1,2},{2,3},{3,4},{4,5},{5,6},{6,7},{7,8},{8,9},{9,10},{10,1... | collective-permute-start | bytes 393224 | tf_op jit(solution)/shard_map/while/body/eval_jaxpr/ppermute | solution.py:18
  145.4 9.3 %collective-permute-start = (bf16[1,8,128,64]{3,2,1,0:T(8,128)(2,1)S(1)}, bf16[1,8,128,64]{3,2,1,0:T(8,128)(2,1)S(1)}, u32[]{:S(2)}, u32[]{:S(2)}) collective-permute-start(bf16[1,8,128,64]{3,2,1,0:T(8,128)(2,1)S(1)} %fusion.67), channel_id=1, source_target_pairs={{0,1},{1,2},{2,3},{3,4},{4,5},{5,6},{6,7},{7,8},{8,9},{9,10},{10,1... | collective-permute-start | bytes 393224 | tf_op jit(solution)/shard_map/while/body/eval_jaxpr/ppermute | solution.py:18
  154.9 9.1 %collective-permute-start = (bf16[1,8,128,64]{3,2,1,0:T(8,128)(2,1)S(1)}, bf16[1,8,128,64]{3,2,1,0:T(8,128)(2,1)S(1)}, u32[]{:S(2)}, u32[]{:S(2)}) collective-permute-start(bf16[1,8,128,64]{3,2,1,0:T(8,128)(2,1)S(1)} %fusion.67), channel_id=1, source_target_pairs={{0,1},{1,2},{2,3},{3,4},{4,5},{5,6},{6,7},{7,8},{8,9},{9,10},{10,1... | collective-permute-start | bytes 393224 | tf_op jit(solution)/shard_map/while/body/eval_jaxpr/ppermute | solution.py:18
  164.2 9.0 %collective-permute-start = (bf16[1,8,128,64]{3,2,1,0:T(8,128)(2,1)S(1)}, bf16[1,8,128,64]{3,2,1,0:T(8,128)(2,1)S(1)}, u32[]{:S(2)}, u32[]{:S(2)}) collective-permute-start(bf16[1,8,128,64]{3,2,1,0:T(8,128)(2,1)S(1)} %fusion.67), channel_id=1, source_target_pairs={{0,1},{1,2},{2,3},{3,4},{4,5},{5,6},{6,7},{7,8},{8,9},{9,10},{10,1... | collective-permute-start | bytes 393224 | tf_op jit(solution)/shard_map/while/body/eval_jaxpr/ppermute | solution.py:18
  173.4 9.4 %collective-permute-start = (bf16[1,8,128,64]{3,2,1,0:T(8,128)(2,1)S(1)}, bf16[1,8,128,64]{3,2,1,0:T(8,128)(2,1)S(1)}, u32[]{:S(2)}, u32[]{:S(2)}) collective-permute-start(bf16[1,8,128,64]{3,2,1,0:T(8,128)(2,1)S(1)} %fusion.67), channel_id=1, source_target_pairs={{0,1},{1,2},{2,3},{3,4},{4,5},{5,6},{6,7},{7,8},{8,9},{9,10},{10,1... | collective-permute-start | bytes 393224 | tf_op jit(solution)/shard_map/while/body/eval_jaxpr/ppermute | solution.py:18
  182.9 9.3 %collective-permute-start = (bf16[1,8,128,64]{3,2,1,0:T(8,128)(2,1)S(1)}, bf16[1,8,128,64]{3,2,1,0:T(8,128)(2,1)S(1)}, u32[]{:S(2)}, u32[]{:S(2)}) collective-permute-start(bf16[1,8,128,64]{3,2,1,0:T(8,128)(2,1)S(1)} %fusion.67), channel_id=1, source_target_pairs={{0,1},{1,2},{2,3},{3,4},{4,5},{5,6},{6,7},{7,8},{8,9},{9,10},{10,1... | collective-permute-start | bytes 393224 | tf_op jit(solution)/shard_map/while/body/eval_jaxpr/ppermute | solution.py:18
  192.5 8.4 %collective-permute-start = (bf16[1,8,128,64]{3,2,1,0:T(8,128)(2,1)S(1)}, bf16[1,8,128,64]{3,2,1,0:T(8,128)(2,1)S(1)}, u32[]{:S(2)}, u32[]{:S(2)}) collective-permute-start(bf16[1,8,128,64]{3,2,1,0:T(8,128)(2,1)S(1)} %fusion.67), channel_id=1, source_target_pairs={{0,1},{1,2},{2,3},{3,4},{4,5},{5,6},{6,7},{7,8},{8,9},{9,10},{10,1... | collective-permute-start | bytes 393224 | tf_op jit(solution)/shard_map/while/body/eval_jaxpr/ppermute | solution.py:18
  201.0 7.7 %collective-permute-start = (bf16[1,8,128,64]{3,2,1,0:T(8,128)(2,1)S(1)}, bf16[1,8,128,64]{3,2,1,0:T(8,128)(2,1)S(1)}, u32[]{:S(2)}, u32[]{:S(2)}) collective-permute-start(bf16[1,8,128,64]{3,2,1,0:T(8,128)(2,1)S(1)} %fusion.67), channel_id=1, source_target_pairs={{0,1},{1,2},{2,3},{3,4},{4,5},{5,6},{6,7},{7,8},{8,9},{9,10},{10,1... | collective-permute-start | bytes 393224 | tf_op jit(solution)/shard_map/while/body/eval_jaxpr/ppermute | solution.py:18
  208.9 7.7 %collective-permute-start = (bf16[1,8,128,64]{3,2,1,0:T(8,128)(2,1)S(1)}, bf16[1,8,128,64]{3,2,1,0:T(8,128)(2,1)S(1)}, u32[]{:S(2)}, u32[]{:S(2)}) collective-permute-start(bf16[1,8,128,64]{3,2,1,0:T(8,128)(2,1)S(1)} %fusion.67), channel_id=1, source_target_pairs={{0,1},{1,2},{2,3},{3,4},{4,5},{5,6},{6,7},{7,8},{8,9},{9,10},{10,1... | collective-permute-start | bytes 393224 | tf_op jit(solution)/shard_map/while/body/eval_jaxpr/ppermute | solution.py:18
  216.8 7.7 %collective-permute-start = (bf16[1,8,128,64]{3,2,1,0:T(8,128)(2,1)S(1)}, bf16[1,8,128,64]{3,2,1,0:T(8,128)(2,1)S(1)}, u32[]{:S(2)}, u32[]{:S(2)}) collective-permute-start(bf16[1,8,128,64]{3,2,1,0:T(8,128)(2,1)S(1)} %fusion.67), channel_id=1, source_target_pairs={{0,1},{1,2},{2,3},{3,4},{4,5},{5,6},{6,7},{7,8},{8,9},{9,10},{10,1... | collective-permute-start | bytes 393224 | tf_op jit(solution)/shard_map/while/body/eval_jaxpr/ppermute | solution.py:18
  224.7 7.7 %collective-permute-start = (bf16[1,8,128,64]{3,2,1,0:T(8,128)(2,1)S(1)}, bf16[1,8,128,64]{3,2,1,0:T(8,128)(2,1)S(1)}, u32[]{:S(2)}, u32[]{:S(2)}) collective-permute-start(bf16[1,8,128,64]{3,2,1,0:T(8,128)(2,1)S(1)} %fusion.67), channel_id=1, source_target_pairs={{0,1},{1,2},{2,3},{3,4},{4,5},{5,6},{6,7},{7,8},{8,9},{9,10},{10,1... | collective-permute-start | bytes 393224 | tf_op jit(solution)/shard_map/while/body/eval_jaxpr/ppermute | solution.py:18
  232.6 7.7 %collective-permute-start = (bf16[1,8,128,64]{3,2,1,0:T(8,128)(2,1)S(1)}, bf16[1,8,128,64]{3,2,1,0:T(8,128)(2,1)S(1)}, u32[]{:S(2)}, u32[]{:S(2)}) collective-permute-start(bf16[1,8,128,64]{3,2,1,0:T(8,128)(2,1)S(1)} %fusion.67), channel_id=1, source_target_pairs={{0,1},{1,2},{2,3},{3,4},{4,5},{5,6},{6,7},{7,8},{8,9},{9,10},{10,1... | collective-permute-start | bytes 393224 | tf_op jit(solution)/shard_map/while/body/eval_jaxpr/ppermute | solution.py:18
  240.5 7.7 %collective-permute-start = (bf16[1,8,128,64]{3,2,1,0:T(8,128)(2,1)S(1)}, bf16[1,8,128,64]{3,2,1,0:T(8,128)(2,1)S(1)}, u32[]{:S(2)}, u32[]{:S(2)}) collective-permute-start(bf16[1,8,128,64]{3,2,1,0:T(8,128)(2,1)S(1)} %fusion.67), channel_id=1, source_target_pairs={{0,1},{1,2},{2,3},{3,4},{4,5},{5,6},{6,7},{7,8},{8,9},{9,10},{10,1... | collective-permute-start | bytes 393224 | tf_op jit(solution)/shard_map/while/body/eval_jaxpr/ppermute | solution.py:18
  248.4 7.7 %collective-permute-start = (bf16[1,8,128,64]{3,2,1,0:T(8,128)(2,1)S(1)}, bf16[1,8,128,64]{3,2,1,0:T(8,128)(2,1)S(1)}, u32[]{:S(2)}, u32[]{:S(2)}) collective-permute-start(bf16[1,8,128,64]{3,2,1,0:T(8,128)(2,1)S(1)} %fusion.67), channel_id=1, source_target_pairs={{0,1},{1,2},{2,3},{3,4},{4,5},{5,6},{6,7},{7,8},{8,9},{9,10},{10,1... | collective-permute-start | bytes 393224 | tf_op jit(solution)/shard_map/while/body/eval_jaxpr/ppermute | solution.py:18
  256.3 7.7 %collective-permute-start = (bf16[1,8,128,64]{3,2,1,0:T(8,128)(2,1)S(1)}, bf16[1,8,128,64]{3,2,1,0:T(8,128)(2,1)S(1)}, u32[]{:S(2)}, u32[]{:S(2)}) collective-permute-start(bf16[1,8,128,64]{3,2,1,0:T(8,128)(2,1)S(1)} %fusion.67), channel_id=1, source_target_pairs={{0,1},{1,2},{2,3},{3,4},{4,5},{5,6},{6,7},{7,8},{8,9},{9,10},{10,1... | collective-permute-start | bytes 393224 | tf_op jit(solution)/shard_map/while/body/eval_jaxpr/ppermute | solution.py:18
  264.1 7.7 %collective-permute-start = (bf16[1,8,128,64]{3,2,1,0:T(8,128)(2,1)S(1)}, bf16[1,8,128,64]{3,2,1,0:T(8,128)(2,1)S(1)}, u32[]{:S(2)}, u32[]{:S(2)}) collective-permute-start(bf16[1,8,128,64]{3,2,1,0:T(8,128)(2,1)S(1)} %fusion.67), channel_id=1, source_target_pairs={{0,1},{1,2},{2,3},{3,4},{4,5},{5,6},{6,7},{7,8},{8,9},{9,10},{10,1... | collective-permute-start | bytes 393224 | tf_op jit(solution)/shard_map/while/body/eval_jaxpr/ppermute | solution.py:18
  272.0 7.7 %collective-permute-start = (bf16[1,8,128,64]{3,2,1,0:T(8,128)(2,1)S(1)}, bf16[1,8,128,64]{3,2,1,0:T(8,128)(2,1)S(1)}, u32[]{:S(2)}, u32[]{:S(2)}) collective-permute-start(bf16[1,8,128,64]{3,2,1,0:T(8,128)(2,1)S(1)} %fusion.67), channel_id=1, source_target_pairs={{0,1},{1,2},{2,3},{3,4},{4,5},{5,6},{6,7},{7,8},{8,9},{9,10},{10,1... | collective-permute-start | bytes 393224 | tf_op jit(solution)/shard_map/while/body/eval_jaxpr/ppermute | solution.py:18
  279.9 7.7 %collective-permute-start = (bf16[1,8,128,64]{3,2,1,0:T(8,128)(2,1)S(1)}, bf16[1,8,128,64]{3,2,1,0:T(8,128)(2,1)S(1)}, u32[]{:S(2)}, u32[]{:S(2)}) collective-permute-start(bf16[1,8,128,64]{3,2,1,0:T(8,128)(2,1)S(1)} %fusion.67), channel_id=1, source_target_pairs={{0,1},{1,2},{2,3},{3,4},{4,5},{5,6},{6,7},{7,8},{8,9},{9,10},{10,1... | collective-permute-start | bytes 393224 | tf_op jit(solution)/shard_map/while/body/eval_jaxpr/ppermute | solution.py:18
  287.8 7.7 %collective-permute-start = (bf16[1,8,128,64]{3,2,1,0:T(8,128)(2,1)S(1)}, bf16[1,8,128,64]{3,2,1,0:T(8,128)(2,1)S(1)}, u32[]{:S(2)}, u32[]{:S(2)}) collective-permute-start(bf16[1,8,128,64]{3,2,1,0:T(8,128)(2,1)S(1)} %fusion.67), channel_id=1, source_target_pairs={{0,1},{1,2},{2,3},{3,4},{4,5},{5,6},{6,7},{7,8},{8,9},{9,10},{10,1... | collective-permute-start | bytes 393224 | tf_op jit(solution)/shard_map/while/body/eval_jaxpr/ppermute | solution.py:18
  295.7 7.7 %collective-permute-start = (bf16[1,8,128,64]{3,2,1,0:T(8,128)(2,1)S(1)}, bf16[1,8,128,64]{3,2,1,0:T(8,128)(2,1)S(1)}, u32[]{:S(2)}, u32[]{:S(2)}) collective-permute-start(bf16[1,8,128,64]{3,2,1,0:T(8,128)(2,1)S(1)} %fusion.67), channel_id=1, source_target_pairs={{0,1},{1,2},{2,3},{3,4},{4,5},{5,6},{6,7},{7,8},{8,9},{9,10},{10,1... | collective-permute-start | bytes 393224 | tf_op jit(solution)/shard_map/while/body/eval_jaxpr/ppermute | solution.py:18
  303.6 7.7 %collective-permute-start = (bf16[1,8,128,64]{3,2,1,0:T(8,128)(2,1)S(1)}, bf16[1,8,128,64]{3,2,1,0:T(8,128)(2,1)S(1)}, u32[]{:S(2)}, u32[]{:S(2)}) collective-permute-start(bf16[1,8,128,64]{3,2,1,0:T(8,128)(2,1)S(1)} %fusion.67), channel_id=1, source_target_pairs={{0,1},{1,2},{2,3},{3,4},{4,5},{5,6},{6,7},{7,8},{8,9},{9,10},{10,1... | collective-permute-start | bytes 393224 | tf_op jit(solution)/shard_map/while/body/eval_jaxpr/ppermute | solution.py:18
  311.5 7.7 %collective-permute-start = (bf16[1,8,128,64]{3,2,1,0:T(8,128)(2,1)S(1)}, bf16[1,8,128,64]{3,2,1,0:T(8,128)(2,1)S(1)}, u32[]{:S(2)}, u32[]{:S(2)}) collective-permute-start(bf16[1,8,128,64]{3,2,1,0:T(8,128)(2,1)S(1)} %fusion.67), channel_id=1, source_target_pairs={{0,1},{1,2},{2,3},{3,4},{4,5},{5,6},{6,7},{7,8},{8,9},{9,10},{10,1... | collective-permute-start | bytes 393224 | tf_op jit(solution)/shard_map/while/body/eval_jaxpr/ppermute | solution.py:18
  319.3 8.5 %collective-permute-start = (bf16[1,8,128,64]{3,2,1,0:T(8,128)(2,1)S(1)}, bf16[1,8,128,64]{3,2,1,0:T(8,128)(2,1)S(1)}, u32[]{:S(2)}, u32[]{:S(2)}) collective-permute-start(bf16[1,8,128,64]{3,2,1,0:T(8,128)(2,1)S(1)} %fusion.67), channel_id=1, source_target_pairs={{0,1},{1,2},{2,3},{3,4},{4,5},{5,6},{6,7},{7,8},{8,9},{9,10},{10,1... | collective-permute-start | bytes 393224 | tf_op jit(solution)/shard_map/while/body/eval_jaxpr/ppermute | solution.py:18
  328.0 8.9 %collective-permute-start = (bf16[1,8,128,64]{3,2,1,0:T(8,128)(2,1)S(1)}, bf16[1,8,128,64]{3,2,1,0:T(8,128)(2,1)S(1)}, u32[]{:S(2)}, u32[]{:S(2)}) collective-permute-start(bf16[1,8,128,64]{3,2,1,0:T(8,128)(2,1)S(1)} %fusion.67), channel_id=1, source_target_pairs={{0,1},{1,2},{2,3},{3,4},{4,5},{5,6},{6,7},{7,8},{8,9},{9,10},{10,1... | collective-permute-start | bytes 393224 | tf_op jit(solution)/shard_map/while/body/eval_jaxpr/ppermute | solution.py:18
  337.1 8.9 %collective-permute-start = (bf16[1,8,128,64]{3,2,1,0:T(8,128)(2,1)S(1)}, bf16[1,8,128,64]{3,2,1,0:T(8,128)(2,1)S(1)}, u32[]{:S(2)}, u32[]{:S(2)}) collective-permute-start(bf16[1,8,128,64]{3,2,1,0:T(8,128)(2,1)S(1)} %fusion.67), channel_id=1, source_target_pairs={{0,1},{1,2},{2,3},{3,4},{4,5},{5,6},{6,7},{7,8},{8,9},{9,10},{10,1... | collective-permute-start | bytes 393224 | tf_op jit(solution)/shard_map/while/body/eval_jaxpr/ppermute | solution.py:18
  346.2 8.9 %collective-permute-start = (bf16[1,8,128,64]{3,2,1,0:T(8,128)(2,1)S(1)}, bf16[1,8,128,64]{3,2,1,0:T(8,128)(2,1)S(1)}, u32[]{:S(2)}, u32[]{:S(2)}) collective-permute-start(bf16[1,8,128,64]{3,2,1,0:T(8,128)(2,1)S(1)} %fusion.67), channel_id=1, source_target_pairs={{0,1},{1,2},{2,3},{3,4},{4,5},{5,6},{6,7},{7,8},{8,9},{9,10},{10,1... | collective-permute-start | bytes 393224 | tf_op jit(solution)/shard_map/while/body/eval_jaxpr/ppermute | solution.py:18
  355.3 8.9 %collective-permute-start = (bf16[1,8,128,64]{3,2,1,0:T(8,128)(2,1)S(1)}, bf16[1,8,128,64]{3,2,1,0:T(8,128)(2,1)S(1)}, u32[]{:S(2)}, u32[]{:S(2)}) collective-permute-start(bf16[1,8,128,64]{3,2,1,0:T(8,128)(2,1)S(1)} %fusion.67), channel_id=1, source_target_pairs={{0,1},{1,2},{2,3},{3,4},{4,5},{5,6},{6,7},{7,8},{8,9},{9,10},{10,1... | collective-permute-start | bytes 393224 | tf_op jit(solution)/shard_map/while/body/eval_jaxpr/ppermute | solution.py:18
  364.4 8.9 %collective-permute-start = (bf16[1,8,128,64]{3,2,1,0:T(8,128)(2,1)S(1)}, bf16[1,8,128,64]{3,2,1,0:T(8,128)(2,1)S(1)}, u32[]{:S(2)}, u32[]{:S(2)}) collective-permute-start(bf16[1,8,128,64]{3,2,1,0:T(8,128)(2,1)S(1)} %fusion.67), channel_id=1, source_target_pairs={{0,1},{1,2},{2,3},{3,4},{4,5},{5,6},{6,7},{7,8},{8,9},{9,10},{10,1... | collective-permute-start | bytes 393224 | tf_op jit(solution)/shard_map/while/body/eval_jaxpr/ppermute | solution.py:18
  373.5 8.9 %collective-permute-start = (bf16[1,8,128,64]{3,2,1,0:T(8,128)(2,1)S(1)}, bf16[1,8,128,64]{3,2,1,0:T(8,128)(2,1)S(1)}, u32[]{:S(2)}, u32[]{:S(2)}) collective-permute-start(bf16[1,8,128,64]{3,2,1,0:T(8,128)(2,1)S(1)} %fusion.67), channel_id=1, source_target_pairs={{0,1},{1,2},{2,3},{3,4},{4,5},{5,6},{6,7},{7,8},{8,9},{9,10},{10,1... | collective-permute-start | bytes 393224 | tf_op jit(solution)/shard_map/while/body/eval_jaxpr/ppermute | solution.py:18
  382.6 8.9 %collective-permute-start = (bf16[1,8,128,64]{3,2,1,0:T(8,128)(2,1)S(1)}, bf16[1,8,128,64]{3,2,1,0:T(8,128)(2,1)S(1)}, u32[]{:S(2)}, u32[]{:S(2)}) collective-permute-start(bf16[1,8,128,64]{3,2,1,0:T(8,128)(2,1)S(1)} %fusion.67), channel_id=1, source_target_pairs={{0,1},{1,2},{2,3},{3,4},{4,5},{5,6},{6,7},{7,8},{8,9},{9,10},{10,1... | collective-permute-start | bytes 393224 | tf_op jit(solution)/shard_map/while/body/eval_jaxpr/ppermute | solution.py:18
  391.7 8.9 %collective-permute-start = (bf16[1,8,128,64]{3,2,1,0:T(8,128)(2,1)S(1)}, bf16[1,8,128,64]{3,2,1,0:T(8,128)(2,1)S(1)}, u32[]{:S(2)}, u32[]{:S(2)}) collective-permute-start(bf16[1,8,128,64]{3,2,1,0:T(8,128)(2,1)S(1)} %fusion.67), channel_id=1, source_target_pairs={{0,1},{1,2},{2,3},{3,4},{4,5},{5,6},{6,7},{7,8},{8,9},{9,10},{10,1... | collective-permute-start | bytes 393224 | tf_op jit(solution)/shard_map/while/body/eval_jaxpr/ppermute | solution.py:18
Sparse Core Ops, SparseCore 0:
  9.4 109.3 all-gather.2
  120.8 83.0 all-gather.4
  408.2 107.0 reduce-scatter.1
where the time goes:
time: 523 us; the launch traced here: 522 us
  waiting for transfers between devices  333 us (64%)
  starting transfers between devices  152 us (29%)
  matrix products  13.5 us (3%)
  between operations  13.3 us (3%)
  other arithmetic  6.76 us (1%)
    ppermute x32, starting transfers between devices, from_behind(): return lax.ppermute(block, axis, route)  152 us
    ppermute x32, waiting for transfers between devices, from_behind(): return lax.ppermute(block, axis, route)  114 us
    all_gather x1, waiting for transfers between devices, per_device(): lax.all_gather(w_in, 'seq', axis=0, tiled=True)  110 us
    reduce_scatter x1, waiting for transfers between devices, per_device(): lax.psum_scatter(terms.astype(jnp.bfloat16), 'dp', scatter_dimension=1, t...  107 us
  transfers between devices with their start and end apart: 35, of which 34 were waited for; matrix products, arithmetic and copies ran while one was open for 3% of the time, Pallas kernels for 0%

commit v1 on v0

--- a/solution.py
+++ b/solution.py
@@ -1,6 +1,10 @@
+import functools
+
 import jax
 import jax.numpy as jnp
 from jax import lax
+from jax.experimental import pallas as pl
+from jax.experimental.pallas import tpu as pltpu
 from jax.sharding import PartitionSpec as P
 
 P_SIZE = 64
@@ -10,6 +14,227 @@
 HG = 8
 XG = 768
 CG = 1288
+ZC = 512
+HALO = 16
+AROWS = 16 + XG
+BF = jnp.bfloat16
+F32 = jnp.float32
+MESH = pl.DeviceIdType.MESH
+VMEM_LIMIT = 56 * 1024 * 1024
+
+A_PARTS = ((0, 400), (400, 384))
+W_PARTS = ((0, 256), (256, 256))
+
+
+class Ring:
+    def __init__(self, buf, parts, chips, core, right, left, sib, sems):
+        self.buf, self.parts, self.chips, self.core = buf, parts, chips, core
+        self.right, self.left, self.sib = right, left, sib
+        self.recv, self.send_r, self.send_l, self.srecv, self.ssend = sems
+        self.half = chips // 2
+
+    def reach(self, h, going_right):
+        return self.half if (h == 0) == going_right else self.half - 1
+
+    def _hop(self, q, to, h, going_right):
+        lo, size = self.parts[h]
+        return pltpu.make_async_remote_copy(
+            src_ref=self.buf.at[q, self.core, pl.ds(lo, size)],
+            dst_ref=self.buf.at[to, self.core, pl.ds(lo, size)],
+            send_sem=(self.send_r if going_right else self.send_l).at[q, h],
+            recv_sem=self.recv.at[to, h],
+            device_id=self.right if going_right else self.left,
+            device_id_type=MESH,
+        )
+
+    def _share(self, q):
+        return pltpu.make_async_remote_copy(
+            src_ref=self.buf.at[q, self.core],
+            dst_ref=self.buf.at[q, self.core],
+            send_sem=self.ssend.at[q],
+            recv_sem=self.srecv.at[q],
+            device_id=self.sib,
+            device_id_type=MESH,
+        )
+
+    def begin(self):
+        for h in range(2):
+            self._hop(0, 1, h, True).start()
+            self._hop(0, self.chips - 1, h, False).start()
+        self._share(0).start()
+
+    def step(self, k, last=False, final=False):
+        z = self.chips
+        for h in range(2):
+            for going_right in (True, False):
+                if final and self.reach(h, going_right) < self.half:
+                    continue
+                q = k if going_right else z - k
+                self._hop(q, q, h, going_right).wait_recv()
+                if final or (last and self.reach(h, going_right) < self.half):
+                    continue
+                self._hop(q, q + 1 if going_right else q - 1, h, going_right).start()
+        self._share(k).start()
+        if not final:
+            self._share(z - k).start()
+
+    def shared(self, q):
+        self._share(q).wait_recv()
+
+    def drain(self):
+        z, half = self.chips, self.half
+
+        def sends(q, going_right, hs):
+            for h in hs:
+                self._hop(q, q, h, going_right).wait_send()
+
+        @pl.loop(0, half - 1)
+        def _(k):
+            sends(k, True, (0, 1))
+            sends(lax.rem(z - k, z), False, (0, 1))
+
+        sends(half - 1, True, (0,))
+        sends(half + 1, False, (1,))
+
+        @pl.loop(0, z)
+        def _(q):
+            self._share(q).wait_send()
+
+
+def ring_sems(chips):
+    dma = pltpu.SemaphoreType.DMA
+    return [dma((chips, 2)), dma((chips, 2)), dma((chips, 2)), dma((chips,)), dma((chips,))]
+
+
+def proj_kernel(chips, tok_hbm, win_ref, proj_ref, dt_ref, tokx, buf_a, buf_z, acc, acc_dt, local_sem, halo_send, halo_recv, *sems):
+    d, s = lax.axis_index("dp"), lax.axis_index("seq")
+    n_seq = 2 * chips
+    core, z = lax.rem(s, 2), s // 2
+    right = (d, lax.rem(s + 2, n_seq))
+    left = (d, lax.rem(s + n_seq - 2, n_seq))
+    sib = (d, s + 1 - 2 * core)
+    nxt = (d, lax.rem(s + 1, n_seq))
+    prv = (d, lax.rem(s + n_seq - 1, n_seq))
+
+    barrier = pltpu.get_barrier_semaphore()
+
+    @pl.loop(1, n_seq)
+    def _(k):
+        pl.semaphore_signal(barrier, inc=1, device_id=(d, lax.rem(s + k, n_seq)), device_id_type=MESH)
+
+    own = pltpu.make_async_copy(tok_hbm, tokx.at[pl.ds(HALO, BLOCK)], local_sem)
+    own.start()
+    buf_a[0, core, 0:16] = jnp.zeros((16, N), BF)
+    dtw = jnp.concatenate([win_ref[:, ZC + XG : CG].astype(F32), jnp.zeros((BLOCK, N - HG), F32)], axis=1)
+    buf_a[0, core, 0:16] = dtw.T[0:16].astype(BF)
+    for t in range(XG // N):
+        buf_a[0, core, 16 + t * N : 16 + (t + 1) * N] = win_ref[:, ZC + t * N : ZC + (t + 1) * N]
+    for t in range(ZC // N):
+        buf_z[0, core, t * N : (t + 1) * N] = win_ref[:, t * N : (t + 1) * N]
+    acc[...] = jnp.zeros_like(acc)
+    acc_dt[...] = jnp.zeros_like(acc_dt)
+    pl.semaphore_wait(barrier, n_seq - 1)
+
+    ring_a = Ring(buf_a, A_PARTS, chips, core, right, left, sib, sems[0:5])
+    ring_z = Ring(buf_z, W_PARTS, chips, core, right, left, sib, sems[5:10])
+    ring_a.begin()
+    halo = pltpu.make_async_remote_copy(
+        src_ref=tok_hbm.at[pl.ds(BLOCK - HALO, HALO)],
+        dst_ref=tokx.at[pl.ds(0, HALO)],
+        send_sem=halo_send,
+        recv_sem=halo_recv,
+        device_id=nxt,
+        device_id_type=MESH,
+    )
+    halo.start()
+    own.wait()
+    halo.wait_recv()
+
+    def tokens_of(q):
+        owner = lax.rem(z - q + chips, chips)
+        return tokx[:, pl.ds(pl.multiple_of(owner * 2 * N, 2 * N), 2 * N)]
+
+    def two_tiles(buf, q, row):
+        left_tile = buf[q, :, row : row + N].reshape(2 * N, N)
+        right_tile = buf[q, :, row + N : row + 2 * N].reshape(2 * N, N)
+        return jnp.concatenate([left_tile, right_tile], axis=1)
+
+    def use_a(q):
+        t = tokens_of(q)
+        w = jnp.concatenate([buf_a[q, 0, 0:16], buf_a[q, 1, 0:16]], axis=1)
+        acc_dt[...] += lax.dot_general(t, w, (((1,), (1,)), ((), ())), preferred_element_type=F32)
+        for i in range(XG // (2 * N)):
+            cols = pl.ds(ZC + i * 2 * N, 2 * N)
+            acc[:, cols] += jnp.dot(t, two_tiles(buf_a, q, 16 + i * 2 * N), preferred_element_type=F32)
+
+    def use_z(q):
+        t = tokens_of(q)
+        for i in range(ZC // (2 * N)):
+            cols = pl.ds(i * 2 * N, 2 * N)
+            acc[:, cols] += jnp.dot(t, two_tiles(buf_z, q, i * 2 * N), preferred_element_type=F32)
+
+    half = chips // 2
+
+    def run(ring, use, after_last):
+        ring.shared(0)
+        use(0)
+
+        def both(k):
+            ring.shared(k)
+            use(k)
+            ring.shared(chips - k)
+            use(chips - k)
+
+        @pl.loop(1, half - 1)
+        def _(k):
+            ring.step(k)
+
+            @pl.when(k > 1)
+            def _():
+                both(k - 1)
+
+        ring.step(half - 1, last=True)
+        after_last()
+        if half > 2:
+            both(half - 2)
+        both(half - 1)
+        ring.step(half, final=True)
+        ring.shared(half)
+        use(half)
+
+    run(ring_a, use_a, ring_z.begin)
+    run(ring_z, use_z, lambda: None)
+    proj_ref[...] = acc[...].astype(BF)
+    dt_ref[...] = acc_dt[...].astype(BF)
+    halo.wait_send()
+    ring_a.drain()
+    ring_z.drain()
+
+
+def project(tokens, w_in, chips):
+    rows = HALO + BLOCK
+    dma = pltpu.SemaphoreType.DMA
+    return pl.pallas_call(
+        functools.partial(proj_kernel, chips),
+        out_shape=(jax.ShapeDtypeStruct((rows, ZC + XG), BF), jax.ShapeDtypeStruct((rows, 16), BF)),
+        in_specs=[pl.BlockSpec(memory_space=pl.ANY), pl.BlockSpec(memory_space=pltpu.VMEM)],
+        out_specs=(pl.BlockSpec(memory_space=pltpu.VMEM), pl.BlockSpec(memory_space=pltpu.VMEM)),
+        scratch_shapes=[
+            pltpu.VMEM((rows, tokens.shape[1]), BF),
+            pltpu.VMEM((chips, 2, AROWS, N), BF),
+            pltpu.VMEM((chips, 2, ZC, N), BF),
+            pltpu.VMEM((rows, ZC + XG), F32),
+            pltpu.VMEM((rows, 16), F32),
+            dma,
+            dma,
+            dma,
+            *ring_sems(chips),
+            *ring_sems(chips),
+        ],
+        compiler_params=pltpu.CompilerParams(
+            collective_id=0, has_side_effects=True, vmem_limit_bytes=VMEM_LIMIT
+        ),
+    )(tokens, w_in)
 
 
 def from_behind(block, axis, distance):
@@ -29,13 +254,13 @@
     heads_dev = decay_rate.shape[0]
     groups_dev = heads_dev // HG
     blocks = rows // BLOCK
-    proj = jnp.dot(
-        tokens, lax.all_gather(w_in, "seq", axis=0, tiled=True), preferred_element_type=jnp.float32
-    )
-    proj = proj.astype(jnp.bfloat16).reshape(rows, groups_dev, CG)
-    xbc = proj[:, :, HG * P_SIZE : HG * P_SIZE + XG]
-    rim = from_behind(xbc[rows - (KCONV - 1) :], "seq", 1)
-    padded = jnp.concatenate([rim, xbc], axis=0).astype(jnp.float32)
+    projx, draw = project(tokens, w_in, lax.axis_size("seq") // 2)
+    draw = draw[HALO:, :HG].astype(jnp.float32)
+    first = lax.axis_index("seq") == 0
+    rim = jnp.where(first, 0, projx[HALO - 3 : HALO, ZC:])
+    xbc = projx[HALO:, ZC:]
+    padded = jnp.concatenate([rim, xbc], axis=0).astype(jnp.float32)[:, None]
+    zpart = projx[HALO:, None, :ZC].astype(jnp.float32)
     taps = conv_weight.reshape(KCONV, groups_dev, XG)
     conv = jnp.zeros((rows, groups_dev, XG), jnp.float32) + conv_bias.reshape(groups_dev, XG)
     for k in range(KCONV):
@@ -44,7 +269,6 @@
     xs = act[:, :, : HG * P_SIZE].reshape(blocks, BLOCK, groups_dev, HG, P_SIZE)
     bmat = act[:, :, HG * P_SIZE : HG * P_SIZE + N].reshape(blocks, BLOCK, groups_dev, N)
     cmat = act[:, :, HG * P_SIZE + N :].reshape(blocks, BLOCK, groups_dev, N)
-    draw = proj[:, :, HG * P_SIZE + XG :].astype(jnp.float32).reshape(rows, heads_dev)
     dt = jax.nn.softplus(draw + dt_bias)
     logdec = (-dt * decay_rate).reshape(blocks, BLOCK, groups_dev, HG)
     dtq = dt.reshape(blocks, BLOCK, groups_dev, HG)
@@ -86,7 +310,6 @@
     yoff = jnp.einsum("btgn,bghnp->btghp", cmat, block_in, precision=lax.Precision.HIGHEST)
     yoff = yoff * jnp.exp(cum)[..., None]
     ys = ydiag + yoff + skip_gain.reshape(groups_dev, HG)[None, None, :, :, None] * xs
-    zpart = proj[:, :, : HG * P_SIZE].astype(jnp.float32)
     gated = ys.reshape(rows, groups_dev, HG * P_SIZE) * jax.nn.silu(zpart)
     meansq = jnp.mean(gated * gated, axis=2, keepdims=True)
     normed = gated * lax.rsqrt(meansq + 1e-05) * norm_gain.reshape(groups_dev, HG * P_SIZE)

time: 523 us -> 503 us (0.962)
  waiting for transfers between devices: 333 us -> 215 us
  Pallas kernels: 0 us -> 108 us
  starting transfers between devices: 152 us -> 145 us
  matrix products: 13.5 us -> 6.77 us
    all_gather x1 -> x0, waiting for transfers between devices: 110 us -> none  [per_device(): lax.all_gather(w_in, 'seq', axis=0, tiled=True)]
    pallas_call x0 -> x1, Pallas kernels: none -> 108 us  [project(): pl.pallas_call(functools.partial(proj_kernel, chips), out_shape=(jax.Shap...]
    ppermute x32 -> x31, waiting for transfers between devices: 114 us -> 102 us  [from_behind(): return lax.ppermute(block, axis, route)]
    ppermute x32 -> x31, starting transfers between devices: 152 us -> 145 us  [from_behind(): return lax.ppermute(block, axis, route)]
    dot_general x1 -> x0, matrix products: 5.67 us -> none  [per_device(): jnp.dot(tokens, lax.all_gather(w_in, 'seq', axis=0, tiled=True), preferre...]
  transfers between devices with their start and end apart: 35 -> 33, of which waited for: 34 -> 32; matrix products, arithmetic and copies ran while one was open for 3% -> 3% of each run, Pallas kernels for 0% -> 22%
where the time goes in v1:
time: 503 us; the launch traced here: 502 us
  waiting for transfers between devices  215 us (43%)
  starting transfers between devices  145 us (29%)
  Pallas kernels  108 us (21%)
  between operations  13.6 us (3%)
  other arithmetic  8.17 us (2%)
  matrix products  6.77 us (1%)
    ppermute x31, starting transfers between devices, from_behind(): return lax.ppermute(block, axis, route)  145 us
    reduce_scatter x1, waiting for transfers between devices, per_device(): lax.psum_scatter(terms.astype(jnp.bfloat16), 'dp', scatter_dimension=1, t...  112 us
    pallas_call x1, Pallas kernels, project(): pl.pallas_call(functools.partial(proj_kernel, chips), out_shape=(jax.Shap...  108 us
    ppermute x31, waiting for transfers between devices, from_behind(): return lax.ppermute(block, axis, route)  102 us
  transfers between devices with their start and end apart: 33, of which 32 were waited for; matrix products, arithmetic and copies ran while one was open for 3% of the time, Pallas kernels for 22%

profile of v1, /device:TPU:1, one launch (start us, length us, event | category | flops | bytes accessed | tf_op | source)
XLA Modules:
  0.0 501.8 jit_solution(6050136051359647732)
XLA Ops:
  9.2 108.1 %shard_map.91 = (bf16[144,1280]{1,0:T(8,128)(2,1)}, bf16[144,16]{1,0:T(8,128)(2,1)}) custom-call(bf16[128,4096]{1,0:T(8,128)(2,1)} %tok_hbm.1, bf16[128,1288]{1,0:T(8,128)(2,1)} %copy.37.win_ref), custom_call_target="tpu_custom_call" | custom-call | tf_op jit(solution)/shard_map/pallas_call | solution.py:217
  123.4 253.3 %while.3 = (s32[]{:T(128)}, f32[1,8,128,64]{3,2,1,0:T(8,128)S(1)}, f32[1,8]{1,0:T(1,128)S(1)}, f32[1,8,128,64]{3,2,1,0:T(8,128)S(1)}, s32[]{:T(128)}, /*index=5*/s32[]{:T(128)}) while((s32[]{:T(128)}, f32[1,8,128,64]{3,2,1,0:T(8,128)S(1)}, f32[1,8]{1,0:T(1,128)S(1)}, f32[1,8,128,64]{3,2,1,0:T(8,128)S(1)}, s32[]{:T(128)}, ...), condition=%wide.region_2.3_spmd.clone, body=%wide.region_1.2_spmd.clone.sunk | while | flops 327683 | bytes 1573015 | solution.py:306
  125.5 3.3 collective-permute-done
  128.9 4.4 collective-permute-start
  133.3 3.3 collective-permute-done
  136.8 4.4 collective-permute-start
  141.2 3.3 collective-permute-done
  144.7 4.4 collective-permute-start
  149.1 3.3 collective-permute-done
  152.6 4.4 collective-permute-start
  157.0 3.3 collective-permute-done
  160.5 4.4 collective-permute-start
  164.9 3.3 collective-permute-done
  168.4 4.4 collective-permute-start
  176.3 4.4 collective-permute-start
  180.6 3.3 collective-permute-done
  184.1 4.4 collective-permute-start
  192.0 4.4 collective-permute-start
  196.4 3.3 collective-permute-done
  199.9 4.4 collective-permute-start
  207.8 4.4 collective-permute-start
  212.2 3.3 collective-permute-done
  215.7 4.4 collective-permute-start
  220.1 3.3 collective-permute-done
  223.6 4.4 collective-permute-start
  228.0 3.3 collective-permute-done
  231.4 4.4 collective-permute-start
  235.8 3.3 collective-permute-done
  239.3 4.4 collective-permute-start
  243.7 3.3 collective-permute-done
  247.2 4.4 collective-permute-start
  251.6 3.3 collective-permute-done
  255.1 4.4 collective-permute-start
  263.0 4.4 collective-permute-start
  270.9 4.4 collective-permute-start
  278.7 4.4 collective-permute-start
  286.6 4.9 collective-permute-start
  295.0 5.6 %collective-permute-start = (bf16[1,8,128,64]{3,2,1,0:T(8,128)(2,1)S(1)}, bf16[1,8,128,64]{3,2,1,0:T(8,128)(2,1)S(1)}, u32[]{:S(2)}, u32[]{:S(2)}) collective-permute-start(bf16[1,8,128,64]{3,2,1,0:T(8,128)(2,1)S(1)} %fusion.47), channel_id=1, source_target_pairs={{0,1},{1,2},{2,3},{3,4},{4,5},{5,6},{6,7},{7,8},{8,9},{9,10},{10,1... | collective-permute-start | bytes 393224 | tf_op jit(solution)/shard_map/while/body/eval_jaxpr/ppermute | solution.py:243
  304.1 5.6 %collective-permute-start = (bf16[1,8,128,64]{3,2,1,0:T(8,128)(2,1)S(1)}, bf16[1,8,128,64]{3,2,1,0:T(8,128)(2,1)S(1)}, u32[]{:S(2)}, u32[]{:S(2)}) collective-permute-start(bf16[1,8,128,64]{3,2,1,0:T(8,128)(2,1)S(1)} %fusion.47), channel_id=1, source_target_pairs={{0,1},{1,2},{2,3},{3,4},{4,5},{5,6},{6,7},{7,8},{8,9},{9,10},{10,1... | collective-permute-start | bytes 393224 | tf_op jit(solution)/shard_map/while/body/eval_jaxpr/ppermute | solution.py:243
  313.2 5.6 %collective-permute-start = (bf16[1,8,128,64]{3,2,1,0:T(8,128)(2,1)S(1)}, bf16[1,8,128,64]{3,2,1,0:T(8,128)(2,1)S(1)}, u32[]{:S(2)}, u32[]{:S(2)}) collective-permute-start(bf16[1,8,128,64]{3,2,1,0:T(8,128)(2,1)S(1)} %fusion.47), channel_id=1, source_target_pairs={{0,1},{1,2},{2,3},{3,4},{4,5},{5,6},{6,7},{7,8},{8,9},{9,10},{10,1... | collective-permute-start | bytes 393224 | tf_op jit(solution)/shard_map/while/body/eval_jaxpr/ppermute | solution.py:243
  322.3 5.6 %collective-permute-start = (bf16[1,8,128,64]{3,2,1,0:T(8,128)(2,1)S(1)}, bf16[1,8,128,64]{3,2,1,0:T(8,128)(2,1)S(1)}, u32[]{:S(2)}, u32[]{:S(2)}) collective-permute-start(bf16[1,8,128,64]{3,2,1,0:T(8,128)(2,1)S(1)} %fusion.47), channel_id=1, source_target_pairs={{0,1},{1,2},{2,3},{3,4},{4,5},{5,6},{6,7},{7,8},{8,9},{9,10},{10,1... | collective-permute-start | bytes 393224 | tf_op jit(solution)/shard_map/while/body/eval_jaxpr/ppermute | solution.py:243
  331.4 5.6 %collective-permute-start = (bf16[1,8,128,64]{3,2,1,0:T(8,128)(2,1)S(1)}, bf16[1,8,128,64]{3,2,1,0:T(8,128)(2,1)S(1)}, u32[]{:S(2)}, u32[]{:S(2)}) collective-permute-start(bf16[1,8,128,64]{3,2,1,0:T(8,128)(2,1)S(1)} %fusion.47), channel_id=1, source_target_pairs={{0,1},{1,2},{2,3},{3,4},{4,5},{5,6},{6,7},{7,8},{8,9},{9,10},{10,1... | collective-permute-start | bytes 393224 | tf_op jit(solution)/shard_map/while/body/eval_jaxpr/ppermute | solution.py:243
  340.5 5.6 %collective-permute-start = (bf16[1,8,128,64]{3,2,1,0:T(8,128)(2,1)S(1)}, bf16[1,8,128,64]{3,2,1,0:T(8,128)(2,1)S(1)}, u32[]{:S(2)}, u32[]{:S(2)}) collective-permute-start(bf16[1,8,128,64]{3,2,1,0:T(8,128)(2,1)S(1)} %fusion.47), channel_id=1, source_target_pairs={{0,1},{1,2},{2,3},{3,4},{4,5},{5,6},{6,7},{7,8},{8,9},{9,10},{10,1... | collective-permute-start | bytes 393224 | tf_op jit(solution)/shard_map/while/body/eval_jaxpr/ppermute | solution.py:243
  349.6 5.6 %collective-permute-start = (bf16[1,8,128,64]{3,2,1,0:T(8,128)(2,1)S(1)}, bf16[1,8,128,64]{3,2,1,0:T(8,128)(2,1)S(1)}, u32[]{:S(2)}, u32[]{:S(2)}) collective-permute-start(bf16[1,8,128,64]{3,2,1,0:T(8,128)(2,1)S(1)} %fusion.47), channel_id=1, source_target_pairs={{0,1},{1,2},{2,3},{3,4},{4,5},{5,6},{6,7},{7,8},{8,9},{9,10},{10,1... | collective-permute-start | bytes 393224 | tf_op jit(solution)/shard_map/while/body/eval_jaxpr/ppermute | solution.py:243
  358.7 5.6 %collective-permute-start = (bf16[1,8,128,64]{3,2,1,0:T(8,128)(2,1)S(1)}, bf16[1,8,128,64]{3,2,1,0:T(8,128)(2,1)S(1)}, u32[]{:S(2)}, u32[]{:S(2)}) collective-permute-start(bf16[1,8,128,64]{3,2,1,0:T(8,128)(2,1)S(1)} %fusion.47), channel_id=1, source_target_pairs={{0,1},{1,2},{2,3},{3,4},{4,5},{5,6},{6,7},{7,8},{8,9},{9,10},{10,1... | collective-permute-start | bytes 393224 | tf_op jit(solution)/shard_map/while/body/eval_jaxpr/ppermute | solution.py:243
  367.8 5.6 %collective-permute-start = (bf16[1,8,128,64]{3,2,1,0:T(8,128)(2,1)S(1)}, bf16[1,8,128,64]{3,2,1,0:T(8,128)(2,1)S(1)}, u32[]{:S(2)}, u32[]{:S(2)}) collective-permute-start(bf16[1,8,128,64]{3,2,1,0:T(8,128)(2,1)S(1)} %fusion.47), channel_id=1, source_target_pairs={{0,1},{1,2},{2,3},{3,4},{4,5},{5,6},{6,7},{7,8},{8,9},{9,10},{10,1... | collective-permute-start | bytes 393224 | tf_op jit(solution)/shard_map/while/body/eval_jaxpr/ppermute | solution.py:243
  379.3 3.9 convolution_convert_fusion
  383.3 111.7 %reduce-scatter.2.cloned.1.call-done = bf16[128,256]{1,0:T(8,128)(2,1)} async-done(((bf16[128,4096]{1,0:T(8,128)(2,1)}), bf16[128,256]{1,0:T(8,128)(2,1)}) %reduce-scatter.2.cloned.1.call-update) | async-done | bytes 65552 | tf_op jit(solution)/shard_map/reduce_scatter | solution.py:320
  (123 shorter events, 74.2 us)
Async XLA Ops:
  6.5 115.9 %copy-start.3 = (f32[8]{0:T(128)S(1)}, f32[8]{0:T(128)}, u32[]{:S(2)}) copy-start(f32[8]{0:T(128)} %param.15) | copy-start | bytes 100
  6.5 372.7 %all-gather.2.cloned.1.call-start = ((), (), s32[]{:S(2)}) async-start(), calls=%async_computation.1 | async-start | bytes 4325376 | tf_op jit(solution)/shard_map/all_gather | solution.py:318
  7.3 487.7 %reduce-scatter.2.cloned.1.call-start = ((), (), s32[]{:S(2)}) async-start(), calls=%async_computation.2 | async-start | bytes 1114112 | tf_op jit(solution)/shard_map/reduce_scatter | solution.py:320
  117.3 5.1 %copy-start.1 = (bf16[144,16]{1,0:T(8,128)(2,1)S(1)}, bf16[144,16]{1,0:T(8,128)(2,1)}, u32[]{:S(2)}) copy-start(bf16[144,16]{1,0:T(8,128)(2,1)} %get-tuple-element.51) | copy-start | bytes 13828
  123.4 254.3 %copy-start.4 = (f32[8]{0:T(128)S(1)}, f32[8]{0:T(128)}, u32[]{:S(2)}) copy-start(f32[8]{0:T(128)} %param.17) | copy-start | bytes 100
  123.4 255.7 %copy-start = (bf16[144,1280]{1,0:T(8,128)(2,1)S(1)}, bf16[144,1280]{1,0:T(8,128)(2,1)}, u32[]{:S(2)}) copy-start(bf16[144,1280]{1,0:T(8,128)(2,1)} %get-tuple-element.50) | copy-start | bytes 1105924
  123.4 255.9 %copy-start.2 = (f32[512]{0:T(512)S(1)}, f32[512]{0:T(512)}, u32[]{:S(2)}) copy-start(f32[512]{0:T(512)} %param.18) | copy-start | bytes 6148
  123.5 5.2 %collective-permute-start = (bf16[1,8,128,64]{3,2,1,0:T(8,128)(2,1)S(1)}, bf16[1,8,128,64]{3,2,1,0:T(8,128)(2,1)S(1)}, u32[]{:S(2)}, u32[]{:S(2)}) collective-permute-start(bf16[1,8,128,64]{3,2,1,0:T(8,128)(2,1)S(1)} %fusion.47), channel_id=1, source_target_pairs={{0,1},{1,2},{2,3},{3,4},{4,5},{5,6},{6,7},{7,8},{8,9},{9,10},{10,1... | collective-permute-start | bytes 393224 | tf_op jit(solution)/shard_map/while/body/eval_jaxpr/ppermute | solution.py:243
  128.9 7.7 %collective-permute-start = (bf16[1,8,128,64]{3,2,1,0:T(8,128)(2,1)S(1)}, bf16[1,8,128,64]{3,2,1,0:T(8,128)(2,1)S(1)}, u32[]{:S(2)}, u32[]{:S(2)}) collective-permute-start(bf16[1,8,128,64]{3,2,1,0:T(8,128)(2,1)S(1)} %fusion.47), channel_id=1, source_target_pairs={{0,1},{1,2},{2,3},{3,4},{4,5},{5,6},{6,7},{7,8},{8,9},{9,10},{10,1... | collective-permute-start | bytes 393224 | tf_op jit(solution)/shard_map/while/body/eval_jaxpr/ppermute | solution.py:243
  136.8 7.7 %collective-permute-start = (bf16[1,8,128,64]{3,2,1,0:T(8,128)(2,1)S(1)}, bf16[1,8,128,64]{3,2,1,0:T(8,128)(2,1)S(1)}, u32[]{:S(2)}, u32[]{:S(2)}) collective-permute-start(bf16[1,8,128,64]{3,2,1,0:T(8,128)(2,1)S(1)} %fusion.47), channel_id=1, source_target_pairs={{0,1},{1,2},{2,3},{3,4},{4,5},{5,6},{6,7},{7,8},{8,9},{9,10},{10,1... | collective-permute-start | bytes 393224 | tf_op jit(solution)/shard_map/while/body/eval_jaxpr/ppermute | solution.py:243
  144.7 7.7 %collective-permute-start = (bf16[1,8,128,64]{3,2,1,0:T(8,128)(2,1)S(1)}, bf16[1,8,128,64]{3,2,1,0:T(8,128)(2,1)S(1)}, u32[]{:S(2)}, u32[]{:S(2)}) collective-permute-start(bf16[1,8,128,64]{3,2,1,0:T(8,128)(2,1)S(1)} %fusion.47), channel_id=1, source_target_pairs={{0,1},{1,2},{2,3},{3,4},{4,5},{5,6},{6,7},{7,8},{8,9},{9,10},{10,1... | collective-permute-start | bytes 393224 | tf_op jit(solution)/shard_map/while/body/eval_jaxpr/ppermute | solution.py:243
  152.6 7.7 %collective-permute-start = (bf16[1,8,128,64]{3,2,1,0:T(8,128)(2,1)S(1)}, bf16[1,8,128,64]{3,2,1,0:T(8,128)(2,1)S(1)}, u32[]{:S(2)}, u32[]{:S(2)}) collective-permute-start(bf16[1,8,128,64]{3,2,1,0:T(8,128)(2,1)S(1)} %fusion.47), channel_id=1, source_target_pairs={{0,1},{1,2},{2,3},{3,4},{4,5},{5,6},{6,7},{7,8},{8,9},{9,10},{10,1... | collective-permute-start | bytes 393224 | tf_op jit(solution)/shard_map/while/body/eval_jaxpr/ppermute | solution.py:243
  160.5 7.7 %collective-permute-start = (bf16[1,8,128,64]{3,2,1,0:T(8,128)(2,1)S(1)}, bf16[1,8,128,64]{3,2,1,0:T(8,128)(2,1)S(1)}, u32[]{:S(2)}, u32[]{:S(2)}) collective-permute-start(bf16[1,8,128,64]{3,2,1,0:T(8,128)(2,1)S(1)} %fusion.47), channel_id=1, source_target_pairs={{0,1},{1,2},{2,3},{3,4},{4,5},{5,6},{6,7},{7,8},{8,9},{9,10},{10,1... | collective-permute-start | bytes 393224 | tf_op jit(solution)/shard_map/while/body/eval_jaxpr/ppermute | solution.py:243
  168.4 7.7 %collective-permute-start = (bf16[1,8,128,64]{3,2,1,0:T(8,128)(2,1)S(1)}, bf16[1,8,128,64]{3,2,1,0:T(8,128)(2,1)S(1)}, u32[]{:S(2)}, u32[]{:S(2)}) collective-permute-start(bf16[1,8,128,64]{3,2,1,0:T(8,128)(2,1)S(1)} %fusion.47), channel_id=1, source_target_pairs={{0,1},{1,2},{2,3},{3,4},{4,5},{5,6},{6,7},{7,8},{8,9},{9,10},{10,1... | collective-permute-start | bytes 393224 | tf_op jit(solution)/shard_map/while/body/eval_jaxpr/ppermute | solution.py:243
  176.3 7.7 %collective-permute-start = (bf16[1,8,128,64]{3,2,1,0:T(8,128)(2,1)S(1)}, bf16[1,8,128,64]{3,2,1,0:T(8,128)(2,1)S(1)}, u32[]{:S(2)}, u32[]{:S(2)}) collective-permute-start(bf16[1,8,128,64]{3,2,1,0:T(8,128)(2,1)S(1)} %fusion.47), channel_id=1, source_target_pairs={{0,1},{1,2},{2,3},{3,4},{4,5},{5,6},{6,7},{7,8},{8,9},{9,10},{10,1... | collective-permute-start | bytes 393224 | tf_op jit(solution)/shard_map/while/body/eval_jaxpr/ppermute | solution.py:243
  184.1 7.7 %collective-permute-start = (bf16[1,8,128,64]{3,2,1,0:T(8,128)(2,1)S(1)}, bf16[1,8,128,64]{3,2,1,0:T(8,128)(2,1)S(1)}, u32[]{:S(2)}, u32[]{:S(2)}) collective-permute-start(bf16[1,8,128,64]{3,2,1,0:T(8,128)(2,1)S(1)} %fusion.47), channel_id=1, source_target_pairs={{0,1},{1,2},{2,3},{3,4},{4,5},{5,6},{6,7},{7,8},{8,9},{9,10},{10,1... | collective-permute-start | bytes 393224 | tf_op jit(solution)/shard_map/while/body/eval_jaxpr/ppermute | solution.py:243
  192.0 7.7 %collective-permute-start = (bf16[1,8,128,64]{3,2,1,0:T(8,128)(2,1)S(1)}, bf16[1,8,128,64]{3,2,1,0:T(8,128)(2,1)S(1)}, u32[]{:S(2)}, u32[]{:S(2)}) collective-permute-start(bf16[1,8,128,64]{3,2,1,0:T(8,128)(2,1)S(1)} %fusion.47), channel_id=1, source_target_pairs={{0,1},{1,2},{2,3},{3,4},{4,5},{5,6},{6,7},{7,8},{8,9},{9,10},{10,1... | collective-permute-start | bytes 393224 | tf_op jit(solution)/shard_map/while/body/eval_jaxpr/ppermute | solution.py:243
  199.9 7.7 %collective-permute-start = (bf16[1,8,128,64]{3,2,1,0:T(8,128)(2,1)S(1)}, bf16[1,8,128,64]{3,2,1,0:T(8,128)(2,1)S(1)}, u32[]{:S(2)}, u32[]{:S(2)}) collective-permute-start(bf16[1,8,128,64]{3,2,1,0:T(8,128)(2,1)S(1)} %fusion.47), channel_id=1, source_target_pairs={{0,1},{1,2},{2,3},{3,4},{4,5},{5,6},{6,7},{7,8},{8,9},{9,10},{10,1... | collective-permute-start | bytes 393224 | tf_op jit(solution)/shard_map/while/body/eval_jaxpr/ppermute | solution.py:243
  207.8 7.7 %collective-permute-start = (bf16[1,8,128,64]{3,2,1,0:T(8,128)(2,1)S(1)}, bf16[1,8,128,64]{3,2,1,0:T(8,128)(2,1)S(1)}, u32[]{:S(2)}, u32[]{:S(2)}) collective-permute-start(bf16[1,8,128,64]{3,2,1,0:T(8,128)(2,1)S(1)} %fusion.47), channel_id=1, source_target_pairs={{0,1},{1,2},{2,3},{3,4},{4,5},{5,6},{6,7},{7,8},{8,9},{9,10},{10,1... | collective-permute-start | bytes 393224 | tf_op jit(solution)/shard_map/while/body/eval_jaxpr/ppermute | solution.py:243
  215.7 7.7 %collective-permute-start = (bf16[1,8,128,64]{3,2,1,0:T(8,128)(2,1)S(1)}, bf16[1,8,128,64]{3,2,1,0:T(8,128)(2,1)S(1)}, u32[]{:S(2)}, u32[]{:S(2)}) collective-permute-start(bf16[1,8,128,64]{3,2,1,0:T(8,128)(2,1)S(1)} %fusion.47), channel_id=1, source_target_pairs={{0,1},{1,2},{2,3},{3,4},{4,5},{5,6},{6,7},{7,8},{8,9},{9,10},{10,1... | collective-permute-start | bytes 393224 | tf_op jit(solution)/shard_map/while/body/eval_jaxpr/ppermute | solution.py:243
  223.6 7.7 %collective-permute-start = (bf16[1,8,128,64]{3,2,1,0:T(8,128)(2,1)S(1)}, bf16[1,8,128,64]{3,2,1,0:T(8,128)(2,1)S(1)}, u32[]{:S(2)}, u32[]{:S(2)}) collective-permute-start(bf16[1,8,128,64]{3,2,1,0:T(8,128)(2,1)S(1)} %fusion.47), channel_id=1, source_target_pairs={{0,1},{1,2},{2,3},{3,4},{4,5},{5,6},{6,7},{7,8},{8,9},{9,10},{10,1... | collective-permute-start | bytes 393224 | tf_op jit(solution)/shard_map/while/body/eval_jaxpr/ppermute | solution.py:243
  231.4 7.7 %collective-permute-start = (bf16[1,8,128,64]{3,2,1,0:T(8,128)(2,1)S(1)}, bf16[1,8,128,64]{3,2,1,0:T(8,128)(2,1)S(1)}, u32[]{:S(2)}, u32[]{:S(2)}) collective-permute-start(bf16[1,8,128,64]{3,2,1,0:T(8,128)(2,1)S(1)} %fusion.47), channel_id=1, source_target_pairs={{0,1},{1,2},{2,3},{3,4},{4,5},{5,6},{6,7},{7,8},{8,9},{9,10},{10,1... | collective-permute-start | bytes 393224 | tf_op jit(solution)/shard_map/while/body/eval_jaxpr/ppermute | solution.py:243
  239.3 7.7 %collective-permute-start = (bf16[1,8,128,64]{3,2,1,0:T(8,128)(2,1)S(1)}, bf16[1,8,128,64]{3,2,1,0:T(8,128)(2,1)S(1)}, u32[]{:S(2)}, u32[]{:S(2)}) collective-permute-start(bf16[1,8,128,64]{3,2,1,0:T(8,128)(2,1)S(1)} %fusion.47), channel_id=1, source_target_pairs={{0,1},{1,2},{2,3},{3,4},{4,5},{5,6},{6,7},{7,8},{8,9},{9,10},{10,1... | collective-permute-start | bytes 393224 | tf_op jit(solution)/shard_map/while/body/eval_jaxpr/ppermute | solution.py:243
  247.2 7.7 %collective-permute-start = (bf16[1,8,128,64]{3,2,1,0:T(8,128)(2,1)S(1)}, bf16[1,8,128,64]{3,2,1,0:T(8,128)(2,1)S(1)}, u32[]{:S(2)}, u32[]{:S(2)}) collective-permute-start(bf16[1,8,128,64]{3,2,1,0:T(8,128)(2,1)S(1)} %fusion.47), channel_id=1, source_target_pairs={{0,1},{1,2},{2,3},{3,4},{4,5},{5,6},{6,7},{7,8},{8,9},{9,10},{10,1... | collective-permute-start | bytes 393224 | tf_op jit(solution)/shard_map/while/body/eval_jaxpr/ppermute | solution.py:243
  255.1 7.7 %collective-permute-start = (bf16[1,8,128,64]{3,2,1,0:T(8,128)(2,1)S(1)}, bf16[1,8,128,64]{3,2,1,0:T(8,128)(2,1)S(1)}, u32[]{:S(2)}, u32[]{:S(2)}) collective-permute-start(bf16[1,8,128,64]{3,2,1,0:T(8,128)(2,1)S(1)} %fusion.47), channel_id=1, source_target_pairs={{0,1},{1,2},{2,3},{3,4},{4,5},{5,6},{6,7},{7,8},{8,9},{9,10},{10,1... | collective-permute-start | bytes 393224 | tf_op jit(solution)/shard_map/while/body/eval_jaxpr/ppermute | solution.py:243
  263.0 7.7 %collective-permute-start = (bf16[1,8,128,64]{3,2,1,0:T(8,128)(2,1)S(1)}, bf16[1,8,128,64]{3,2,1,0:T(8,128)(2,1)S(1)}, u32[]{:S(2)}, u32[]{:S(2)}) collective-permute-start(bf16[1,8,128,64]{3,2,1,0:T(8,128)(2,1)S(1)} %fusion.47), channel_id=1, source_target_pairs={{0,1},{1,2},{2,3},{3,4},{4,5},{5,6},{6,7},{7,8},{8,9},{9,10},{10,1... | collective-permute-start | bytes 393224 | tf_op jit(solution)/shard_map/while/body/eval_jaxpr/ppermute | solution.py:243
  270.9 7.7 %collective-permute-start = (bf16[1,8,128,64]{3,2,1,0:T(8,128)(2,1)S(1)}, bf16[1,8,128,64]{3,2,1,0:T(8,128)(2,1)S(1)}, u32[]{:S(2)}, u32[]{:S(2)}) collective-permute-start(bf16[1,8,128,64]{3,2,1,0:T(8,128)(2,1)S(1)} %fusion.47), channel_id=1, source_target_pairs={{0,1},{1,2},{2,3},{3,4},{4,5},{5,6},{6,7},{7,8},{8,9},{9,10},{10,1... | collective-permute-start | bytes 393224 | tf_op jit(solution)/shard_map/while/body/eval_jaxpr/ppermute | solution.py:243
  278.7 7.7 %collective-permute-start = (bf16[1,8,128,64]{3,2,1,0:T(8,128)(2,1)S(1)}, bf16[1,8,128,64]{3,2,1,0:T(8,128)(2,1)S(1)}, u32[]{:S(2)}, u32[]{:S(2)}) collective-permute-start(bf16[1,8,128,64]{3,2,1,0:T(8,128)(2,1)S(1)} %fusion.47), channel_id=1, source_target_pairs={{0,1},{1,2},{2,3},{3,4},{4,5},{5,6},{6,7},{7,8},{8,9},{9,10},{10,1... | collective-permute-start | bytes 393224 | tf_op jit(solution)/shard_map/while/body/eval_jaxpr/ppermute | solution.py:243
  286.6 8.2 %collective-permute-start = (bf16[1,8,128,64]{3,2,1,0:T(8,128)(2,1)S(1)}, bf16[1,8,128,64]{3,2,1,0:T(8,128)(2,1)S(1)}, u32[]{:S(2)}, u32[]{:S(2)}) collective-permute-start(bf16[1,8,128,64]{3,2,1,0:T(8,128)(2,1)S(1)} %fusion.47), channel_id=1, source_target_pairs={{0,1},{1,2},{2,3},{3,4},{4,5},{5,6},{6,7},{7,8},{8,9},{9,10},{10,1... | collective-permute-start | bytes 393224 | tf_op jit(solution)/shard_map/while/body/eval_jaxpr/ppermute | solution.py:243
  295.0 8.9 %collective-permute-start = (bf16[1,8,128,64]{3,2,1,0:T(8,128)(2,1)S(1)}, bf16[1,8,128,64]{3,2,1,0:T(8,128)(2,1)S(1)}, u32[]{:S(2)}, u32[]{:S(2)}) collective-permute-start(bf16[1,8,128,64]{3,2,1,0:T(8,128)(2,1)S(1)} %fusion.47), channel_id=1, source_target_pairs={{0,1},{1,2},{2,3},{3,4},{4,5},{5,6},{6,7},{7,8},{8,9},{9,10},{10,1... | collective-permute-start | bytes 393224 | tf_op jit(solution)/shard_map/while/body/eval_jaxpr/ppermute | solution.py:243
  304.1 8.9 %collective-permute-start = (bf16[1,8,128,64]{3,2,1,0:T(8,128)(2,1)S(1)}, bf16[1,8,128,64]{3,2,1,0:T(8,128)(2,1)S(1)}, u32[]{:S(2)}, u32[]{:S(2)}) collective-permute-start(bf16[1,8,128,64]{3,2,1,0:T(8,128)(2,1)S(1)} %fusion.47), channel_id=1, source_target_pairs={{0,1},{1,2},{2,3},{3,4},{4,5},{5,6},{6,7},{7,8},{8,9},{9,10},{10,1... | collective-permute-start | bytes 393224 | tf_op jit(solution)/shard_map/while/body/eval_jaxpr/ppermute | solution.py:243
  313.2 8.9 %collective-permute-start = (bf16[1,8,128,64]{3,2,1,0:T(8,128)(2,1)S(1)}, bf16[1,8,128,64]{3,2,1,0:T(8,128)(2,1)S(1)}, u32[]{:S(2)}, u32[]{:S(2)}) collective-permute-start(bf16[1,8,128,64]{3,2,1,0:T(8,128)(2,1)S(1)} %fusion.47), channel_id=1, source_target_pairs={{0,1},{1,2},{2,3},{3,4},{4,5},{5,6},{6,7},{7,8},{8,9},{9,10},{10,1... | collective-permute-start | bytes 393224 | tf_op jit(solution)/shard_map/while/body/eval_jaxpr/ppermute | solution.py:243
  322.3 8.9 %collective-permute-start = (bf16[1,8,128,64]{3,2,1,0:T(8,128)(2,1)S(1)}, bf16[1,8,128,64]{3,2,1,0:T(8,128)(2,1)S(1)}, u32[]{:S(2)}, u32[]{:S(2)}) collective-permute-start(bf16[1,8,128,64]{3,2,1,0:T(8,128)(2,1)S(1)} %fusion.47), channel_id=1, source_target_pairs={{0,1},{1,2},{2,3},{3,4},{4,5},{5,6},{6,7},{7,8},{8,9},{9,10},{10,1... | collective-permute-start | bytes 393224 | tf_op jit(solution)/shard_map/while/body/eval_jaxpr/ppermute | solution.py:243
  331.4 8.9 %collective-permute-start = (bf16[1,8,128,64]{3,2,1,0:T(8,128)(2,1)S(1)}, bf16[1,8,128,64]{3,2,1,0:T(8,128)(2,1)S(1)}, u32[]{:S(2)}, u32[]{:S(2)}) collective-permute-start(bf16[1,8,128,64]{3,2,1,0:T(8,128)(2,1)S(1)} %fusion.47), channel_id=1, source_target_pairs={{0,1},{1,2},{2,3},{3,4},{4,5},{5,6},{6,7},{7,8},{8,9},{9,10},{10,1... | collective-permute-start | bytes 393224 | tf_op jit(solution)/shard_map/while/body/eval_jaxpr/ppermute | solution.py:243
  340.5 8.9 %collective-permute-start = (bf16[1,8,128,64]{3,2,1,0:T(8,128)(2,1)S(1)}, bf16[1,8,128,64]{3,2,1,0:T(8,128)(2,1)S(1)}, u32[]{:S(2)}, u32[]{:S(2)}) collective-permute-start(bf16[1,8,128,64]{3,2,1,0:T(8,128)(2,1)S(1)} %fusion.47), channel_id=1, source_target_pairs={{0,1},{1,2},{2,3},{3,4},{4,5},{5,6},{6,7},{7,8},{8,9},{9,10},{10,1... | collective-permute-start | bytes 393224 | tf_op jit(solution)/shard_map/while/body/eval_jaxpr/ppermute | solution.py:243
  349.6 8.9 %collective-permute-start = (bf16[1,8,128,64]{3,2,1,0:T(8,128)(2,1)S(1)}, bf16[1,8,128,64]{3,2,1,0:T(8,128)(2,1)S(1)}, u32[]{:S(2)}, u32[]{:S(2)}) collective-permute-start(bf16[1,8,128,64]{3,2,1,0:T(8,128)(2,1)S(1)} %fusion.47), channel_id=1, source_target_pairs={{0,1},{1,2},{2,3},{3,4},{4,5},{5,6},{6,7},{7,8},{8,9},{9,10},{10,1... | collective-permute-start | bytes 393224 | tf_op jit(solution)/shard_map/while/body/eval_jaxpr/ppermute | solution.py:243
  358.7 8.9 %collective-permute-start = (bf16[1,8,128,64]{3,2,1,0:T(8,128)(2,1)S(1)}, bf16[1,8,128,64]{3,2,1,0:T(8,128)(2,1)S(1)}, u32[]{:S(2)}, u32[]{:S(2)}) collective-permute-start(bf16[1,8,128,64]{3,2,1,0:T(8,128)(2,1)S(1)} %fusion.47), channel_id=1, source_target_pairs={{0,1},{1,2},{2,3},{3,4},{4,5},{5,6},{6,7},{7,8},{8,9},{9,10},{10,1... | collective-permute-start | bytes 393224 | tf_op jit(solution)/shard_map/while/body/eval_jaxpr/ppermute | solution.py:243
  367.8 8.9 %collective-permute-start = (bf16[1,8,128,64]{3,2,1,0:T(8,128)(2,1)S(1)}, bf16[1,8,128,64]{3,2,1,0:T(8,128)(2,1)S(1)}, u32[]{:S(2)}, u32[]{:S(2)}) collective-permute-start(bf16[1,8,128,64]{3,2,1,0:T(8,128)(2,1)S(1)} %fusion.47), channel_id=1, source_target_pairs={{0,1},{1,2},{2,3},{3,4},{4,5},{5,6},{6,7},{7,8},{8,9},{9,10},{10,1... | collective-permute-start | bytes 393224 | tf_op jit(solution)/shard_map/while/body/eval_jaxpr/ppermute | solution.py:243
Sparse Core Ops, SparseCore 0:
  9.4 104.5 all-gather.1
  383.4 111.5 reduce-scatter.1

commit v2 on v1

v2 whole, which is shorter than its diff:
```python
import functools

import jax
import jax.numpy as jnp
from jax import lax
from jax.experimental import pallas as pl
from jax.experimental.pallas import tpu as pltpu
from jax.sharding import PartitionSpec as P

P_SIZE = 64
N = 128
KCONV = 4
BLOCK = 128
HG = 8
XG = 768
CG = 1288
ZC = 512
HALO = 16
AROWS = 16 + XG
XT = ZC // N
BF = jnp.bfloat16
F32 = jnp.float32
MESH = pl.DeviceIdType.MESH
HIGHEST = lax.Precision.HIGHEST
VMEM_LIMIT = 56 * 1024 * 1024

A_PARTS = ((0, 400), (400, 384))
W_PARTS = ((0, 256), (256, 256))


class Ring:
    def __init__(self, buf, parts, chips, core, right, left, sib, sems):
        self.buf, self.parts, self.chips, self.core = buf, parts, chips, core
        self.right, self.left, self.sib = right, left, sib
        self.recv, self.send_r, self.send_l, self.srecv, self.ssend = sems
        self.half = chips // 2

    def reach(self, h, going_right):
        return self.half if (h == 0) == going_right else self.half - 1

    def _hop(self, q, to, h, going_right):
        lo, size = self.parts[h]
        return pltpu.make_async_remote_copy(
            src_ref=self.buf.at[q, self.core, pl.ds(lo, size)],
            dst_ref=self.buf.at[to, self.core, pl.ds(lo, size)],
            send_sem=(self.send_r if going_right else self.send_l).at[q, h],
            recv_sem=self.recv.at[to, h],
            device_id=self.right if going_right else self.left,
            device_id_type=MESH,
        )

    def _share(self, q):
        return pltpu.make_async_remote_copy(
            src_ref=self.buf.at[q, self.core],
            dst_ref=self.buf.at[q, self.core],
            send_sem=self.ssend.at[q],
            recv_sem=self.srecv.at[q],
            device_id=self.sib,
            device_id_type=MESH,
        )

    def begin(self):
        for h in range(2):
            self._hop(0, 1, h, True).start()
            self._hop(0, self.chips - 1, h, False).start()
        self._share(0).start()

    def step(self, k, last=False, final=False):
        z = self.chips
        for h in range(2):
            for going_right in (True, False):
                if final and self.reach(h, going_right) < self.half:
                    continue
                q = k if going_right else z - k
                self._hop(q, q, h, going_right).wait_recv()
                if final or (last and self.reach(h, going_right) < self.half):
                    continue
                self._hop(q, q + 1 if going_right else q - 1, h, going_right).start()
        self._share(k).start()
        if not final:
            self._share(z - k).start()

    def at(self, k):
        self.step(k, last=k == self.half - 1, final=k == self.half)

    def shared(self, q):
        self._share(q).wait_recv()

    def drain(self):
        z, half = self.chips, self.half

        def sends(q, going_right, hs):
            for h in hs:
                self._hop(q, q, h, going_right).wait_send()

        @pl.loop(0, half - 1)
        def _(k):
            sends(k, True, (0, 1))
            sends(lax.rem(z - k, z), False, (0, 1))

        sends(half - 1, True, (0,))
        sends(half + 1, False, (1,))

        @pl.loop(0, z)
        def _(q):
            self._share(q).wait_send()


def ring_sems(chips):
    dma = pltpu.SemaphoreType.DMA
    return [dma((chips, 2)), dma((chips, 2)), dma((chips, 2)), dma((chips,)), dma((chips,))]


class Exchange:
    def __init__(self, out, inn, chips, z, peer, send, recv):
        self.out, self.inn, self.chips, self.z, self.peer = out, inn, chips, z, peer
        self.send, self.recv = send, recv
        half = chips // 2
        self.order = [half] + [k for j in range(1, half) for k in (half - j, half + j)]

    def _copy(self, o, slot):
        return pltpu.make_async_remote_copy(
            src_ref=self.out.at[o],
            dst_ref=self.inn.at[slot],
            send_sem=self.send.at[o],
            recv_sem=self.recv.at[slot],
            device_id=self.peer(o),
            device_id_type=MESH,
        )

    def begin(self):
        for k in self.order:
            self._copy(lax.rem(self.z + k, self.chips), self.z).start()
        self.inn[self.z] = self.out[self.z]

    def arrive(self):
        for k in reversed(self.order):
            q = lax.rem(self.z + k, self.chips)
            self._copy(q, q).wait_recv()

    def drain(self):
        for k in self.order:
            q = lax.rem(self.z + k, self.chips)
            self._copy(q, q).wait_send()


def silu(v):
    return v / (1.0 + jnp.exp(-v))


def two_parts(row):
    shape = (16, row.shape[1])
    high = row.astype(BF).astype(F32)
    low = row - high
    at = lax.broadcasted_iota(jnp.int32, shape, 0)
    high, low = jnp.broadcast_to(high, shape), jnp.broadcast_to(low, shape)
    return jnp.where(at == 0, high, jnp.where(at == 1, low, 0.0)).astype(BF)


def one_row(tile):
    tile = tile.astype(F32)
    return tile[0:1] + tile[1:2]


def head_lanes(values, j):
    shape = (values.shape[0], N)
    lane = lax.broadcasted_iota(jnp.int32, shape, 1)
    first = jnp.broadcast_to(values[:, 2 * j : 2 * j + 1], shape)
    second = jnp.broadcast_to(values[:, 2 * j + 1 : 2 * j + 2], shape)
    return jnp.where(lane < P_SIZE, first, second)


def batches(half):
    if half < 4:
        return [(0, half - 1), (half, half)]
    return [(0, half // 2), (half // 2 + 1, half - 2), (half - 1, half)]


def mixer_kernel(
    chips, n_dp,
    tok_hbm, win_ref, taps_ref, cbias_ref, dtb_ref, rate_ref, skip_ref, gain_ref, wout_ref,
    out_ref,
    tokx, buf_a, buf_z, buf_o, acc, acc_dt, xf, x1_out, x1_in, st_out, st_in, hin_out, hin_in,
    x2_out, hfull, normed, t_out, r_in,
    local_sem, halo_send, halo_recv, x1_send, x1_recv, x2_send, x2_recv,
    e1_send, e1_recv, e2_send, e2_recv, rs_send, rs_recv, *sems,
):
    d, s = lax.axis_index("dp"), lax.axis_index("seq")
    n_seq = 2 * chips
    half = chips // 2
    core, z = lax.rem(s, 2), s // 2
    right = (d, lax.rem(s + 2, n_seq))
    left = (d, lax.rem(s + n_seq - 2, n_seq))
    sib = (d, s + 1 - 2 * core)
    nxt = (d, lax.rem(s + 1, n_seq))
    odd = (d, lax.rem(s + n_seq - 1 + 2 * core, n_seq))
    tile_rows = 2 * N // chips

    barrier = pltpu.get_barrier_semaphore()

    def greet(device):
        pl.semaphore_signal(barrier, inc=1, device_id=device, device_id_type=MESH)

    @pl.loop(1, chips)
    def _(k):
        greet((d, lax.rem(s + 2 * k, n_seq)))

    @pl.loop(1, n_dp)
    def _(k):
        greet((lax.rem(d + k, n_dp), s))

    greet(sib)
    greet(odd)

    own = pltpu.make_async_copy(tok_hbm, tokx.at[pl.ds(HALO, BLOCK)], local_sem)
    own.start()
    dtw = jnp.concatenate([win_ref[:, ZC + XG : CG].astype(F32), jnp.zeros((BLOCK, N - HG), F32)], axis=1)
    buf_a[0, core, 0:16] = dtw.T[0:16].astype(BF)
    for t in range(XG // N):
        buf_a[0, core, 16 + t * N : 16 + (t + 1) * N] = win_ref[:, ZC + t * N : ZC + (t + 1) * N]
    for t in range(XT):
        buf_z[0, core, t * N : (t + 1) * N] = win_ref[:, t * N : (t + 1) * N]
    buf_o[0, core] = wout_ref[...]
    acc[...] = jnp.zeros_like(acc)
    acc_dt[...] = jnp.zeros_like(acc_dt)
    pl.semaphore_wait(barrier, chips + n_dp)

    ring_a = Ring(buf_a, A_PARTS, chips, core, right, left, sib, sems[0:5])
    ring_z = Ring(buf_z, W_PARTS, chips, core, right, left, sib, sems[5:10])
    ring_o = Ring(buf_o, W_PARTS, chips, core, right, left, sib, sems[10:15])
    ring_a.begin()
    halo = pltpu.make_async_remote_copy(
        src_ref=tok_hbm.at[pl.ds(BLOCK - HALO, HALO)],
        dst_ref=tokx.at[pl.ds(0, HALO)],
        send_sem=halo_send,
        recv_sem=halo_recv,
        device_id=nxt,
        device_id_type=MESH,
    )
    halo.start()
    own.wait()
    halo.wait_recv()

    def columns_of(q):
        owner = lax.rem(z - q + chips, chips)
        return pl.ds(pl.multiple_of(owner * 2 * N, 2 * N), 2 * N)

    def two_tiles(buf, q, row):
        left_tile = buf[q, :, row : row + N].reshape(2 * N, N)
        right_tile = buf[q, :, row + N : row + 2 * N].reshape(2 * N, N)
        return jnp.concatenate([left_tile, right_tile], axis=1)

    def use_a(q):
        ring_a.shared(q)
        t = tokx[:, columns_of(q)]
        w = jnp.concatenate([buf_a[q, 0, 0:16], buf_a[q, 1, 0:16]], axis=1)
        acc_dt[...] += lax.dot_general(t, w, (((1,), (1,)), ((), ())), preferred_element_type=F32)
        for i in range(XG // (2 * N)):
            cols = pl.ds(ZC + i * 2 * N, 2 * N)
            acc[:, cols] += jnp.dot(t, two_tiles(buf_a, q, 16 + i * 2 * N), preferred_element_type=F32)

    def use_z(q):
        ring_z.shared(q)
        t = tokx[HALO:, columns_of(q)]
        for i in range(ZC // (2 * N)):
            cols = pl.ds(i * 2 * N, 2 * N)
            acc[HALO:, cols] += jnp.dot(t, two_tiles(buf_z, q, i * 2 * N), preferred_element_type=F32)

    use_a(0)

    @pl.loop(1, half - 1)
    def _(k):
        ring_a.step(k)

        @pl.when(k > 1)
        def _():
            use_a(k - 1)
            use_a(chips - k + 1)

    ring_a.at(half - 1)
    ring_z.begin()
    ring_o.begin()
    if half > 2:
        use_a(half - 2)
        use_a(half + 2)
    use_a(half - 1)
    use_a(half + 1)
    ring_a.at(half)
    done_z, done_o = [0], [0]

    def more_z(n=1):
        for _ in range(n):
            if done_z[0] < half:
                done_z[0] += 1
                ring_z.at(done_z[0])

    def more_o(n=1):
        for _ in range(n):
            if done_o[0] < half:
                done_o[0] += 1
                ring_o.at(done_o[0])

    used_z = [-1]

    def use_z_to(k):
        while used_z[0] < min(k, half):
            used_z[0] += 1
            use_z(used_z[0])
            if 0 < used_z[0] < half:
                use_z(chips - used_z[0])

    more_z()
    use_a(half)

    keep = jnp.where(s == 0, 0.0, 1.0)
    act = []
    for t in range(XG // N):
        cols = slice(t * N, (t + 1) * N)
        xbc = acc[:, ZC + t * N : ZC + (t + 1) * N].astype(BF).astype(F32)
        xf[0:HALO, cols] = xbc[0:HALO] * keep
        xf[HALO:, cols] = xbc[HALO:]
        conv = jnp.broadcast_to(cbias_ref[0:1, cols], (BLOCK, N))
        for k in range(KCONV):
            start = HALO - KCONV + 1 + k
            conv = conv + taps_ref[k : k + 1, cols] * xf[start : start + BLOCK, cols]
        act.append(silu(conv))
    xs, bmat, cmat = act[:XT], act[XT], act[XT + 1]

    draw = acc_dt[HALO:, 0:HG].astype(BF).astype(F32) + dtb_ref[0:1, :]
    dt = jnp.maximum(draw, 0.0) + jnp.log1p(jnp.exp(-jnp.abs(draw)))
    rows = lax.broadcasted_iota(jnp.int32, (BLOCK, BLOCK), 0)
    cols = lax.broadcasted_iota(jnp.int32, (BLOCK, BLOCK), 1)
    causal = rows >= cols
    cum = jnp.dot(
        causal.astype(F32), -dt * rate_ref[0:1, :], preferred_element_type=F32, precision=HIGHEST
    )
    cum_rows = jnp.concatenate([cum, jnp.zeros((BLOCK, N - HG), F32)], axis=1).T
    end = cum[BLOCK - 1 : BLOCK]
    tail = jnp.exp(end - cum)
    whole = jnp.exp(end)

    more_z()

    b_turned = bmat.T.astype(BF)
    dosed = [xs[j] * head_lanes(dt, j) for j in range(XT)]
    states = [
        jnp.dot(b_turned, (dosed[j] * head_lanes(tail, j)).astype(BF), preferred_element_type=F32)
        for j in range(XT)
    ]
    fades = [head_lanes(whole, j) for j in range(XT)]
    pair = XT // 2
    first_core = core == 0

    def joined(parts):
        return jnp.concatenate(parts, axis=1)

    low_state, high_state = joined(states[:pair]), joined(states[pair:])
    low_fade, high_fade = joined(fades[:pair]), joined(fades[pair:])
    kept = jnp.where(first_core, low_state, high_state)
    kept_fade = jnp.where(first_core, low_fade, high_fade)
    x1_out[0:N] = jnp.where(first_core, high_state, low_state).astype(BF)
    x1_out[N : N + 16] = two_parts(jnp.where(first_core, high_fade, low_fade))
    swap1 = pltpu.make_async_remote_copy(
        src_ref=x1_out, dst_ref=x1_in, send_sem=x1_send, recv_sem=x1_recv,
        device_id=sib, device_id_type=MESH,
    )
    swap1.start()

    more_z()

    scores = lax.dot_general(
        cmat.astype(BF), bmat.astype(BF), (((1,), (1,)), ((), ())), preferred_element_type=F32
    )
    lane = lax.broadcasted_iota(jnp.int32, (BLOCK, N), 1)

    def inner(j):
        mix = []
        for h in (2 * j, 2 * j + 1):
            gap = jnp.where(causal, cum[:, h : h + 1] - cum_rows[h : h + 1, :], -1e30)
            mix.append((jnp.exp(gap) * scores).astype(BF))
        low = jnp.where(lane < P_SIZE, dosed[j], 0.0).astype(BF)
        high = jnp.where(lane < P_SIZE, 0.0, dosed[j]).astype(BF)
        y = jnp.dot(
            jnp.concatenate(mix, axis=1), jnp.concatenate([low, high], axis=0),
            preferred_element_type=F32,
        )
        return y + head_lanes(skip_ref[0:1, :], j) * xs[j]

    ys = [inner(j) for j in range(pair)]

    swap1.wait_recv()
    other = x1_in[0:N].astype(F32)
    other_fade = one_row(x1_in[N : N + 16])
    state0 = jnp.where(first_core, kept, other)
    state1 = jnp.where(first_core, other, kept)
    fade0 = jnp.where(first_core, kept_fade, other_fade)
    fade1 = jnp.where(first_core, other_fade, kept_fade)
    chip_state = (state0 * fade1 + state1).astype(BF)
    chip_fade = two_parts(fade0 * fade1)
    for o in range(chips):
        i, j = o % half, o // half
        st_out[o, 0:tile_rows] = chip_state[i * tile_rows : (i + 1) * tile_rows, j * N : (j + 1) * N]
        st_out[o, tile_rows : tile_rows + 16] = chip_fade[:, j * N : (j + 1) * N]

    def peer(o):
        return (d, 2 * o + core)

    gather_states = Exchange(st_out, st_in, chips, z, peer, e1_send, e1_recv)
    gather_states.begin()

    more_z()
    more_o()
    ys += [inner(j) for j in range(pair, XT)]
    use_z_to(2)
    more_z()

    gather_states.arrive()
    carry = jnp.zeros((tile_rows, N), F32)
    for q in range(chips):
        hin_out[q] = carry.astype(BF)
        carry = carry * one_row(st_in[q, tile_rows : tile_rows + 16]) + st_in[q, 0:tile_rows].astype(F32)
    return_states = Exchange(hin_out, hin_in, chips, z, peer, e2_send, e2_recv)
    return_states.begin()

    more_o()
    more_z()
    use_z_to(4)

    return_states.arrive()
    entry = joined([hin_in[j * half : (j + 1) * half].reshape(N, N) for j in range(pair)]).astype(F32)
    middle = entry * fade0 + state0
    x2_out[...] = jnp.where(first_core, middle, entry).astype(BF)
    swap2 = pltpu.make_async_remote_copy(
        src_ref=x2_out, dst_ref=hfull.at[core], send_sem=x2_send, recv_sem=x2_recv,
        device_id=sib, device_id_type=MESH,
    )
    swap2.start()
    hfull[core] = jnp.where(first_core, entry, middle).astype(BF)

    more_z()
    use_z_to(6)
    more_o()
    more_z(half)
    use_z_to(half)
    swap2.wait_recv()

    grown = jnp.exp(cum)
    c_half = cmat.astype(BF)
    gated = []
    square = jnp.zeros((BLOCK, 1), F32)
    for j in range(XT):
        h_in = hfull[j // pair, :, (j % pair) * N : (j % pair + 1) * N]
        y = ys[j] + head_lanes(grown, j) * jnp.dot(c_half, h_in, preferred_element_type=F32)
        g = y * silu(acc[HALO:, j * N : (j + 1) * N].astype(BF).astype(F32))
        square = square + jnp.sum(g * g, axis=1, keepdims=True)
        gated.append(g)
    scale = lax.rsqrt(square / ZC + 1e-05)
    for j in range(XT):
        normed[:, j * N : (j + 1) * N] = (gated[j] * scale * gain_ref[0:1, j * N : (j + 1) * N]).astype(BF)

    def send_term(o, q, slot):
        return pltpu.make_async_remote_copy(
            src_ref=t_out.at[q], dst_ref=r_in.at[slot], send_sem=rs_send.at[q], recv_sem=rs_recv.at[slot],
            device_id=(o, s), device_id_type=MESH,
        )

    def term(q):
        ring_o.shared(q)
        w = jnp.concatenate([buf_o[q, 0], buf_o[q, 1]], axis=1)
        value = jnp.dot(normed[...], w, preferred_element_type=F32).astype(BF)
        o = lax.rem(z - q + chips, chips)
        t_out[q] = value

        @pl.when(o != d)
        def _():
            send_term(o, q, d).start()

        @pl.when(o == d)
        def _():
            r_in[d] = value

    for lo, hi in batches(half):
        more_o(hi - done_o[0])
        steps = hi - lo + 1
        count = 2 * hi + 1 if lo == 0 else (2 * (half - lo) + 1 if hi == half else 2 * steps)

        @pl.loop(0, count)
        def _(i):
            at = lax.rem(i + d, count)
            if lo == 0:
                term(lax.rem(at - hi + chips, chips))
            elif hi == half:
                term(lo + at)
            else:
                term(jnp.where(at < steps, lo + at, chips - hi + at - steps))

    total = jnp.zeros((BLOCK, 2 * N), F32)

    @pl.loop(1, n_dp)
    def _(k):
        e = lax.rem(d + k, n_dp)
        send_term(e, e, e).wait_recv()

    for e in range(n_dp):
        total = total + r_in[e].astype(F32)
    out_ref[...] = total.astype(BF)

    @pl.loop(0, chips)
    def _(q):
        o = lax.rem(z - q + chips, chips)

        @pl.when(o != d)
        def _():
            send_term(o, q, d).wait_send()

    halo.wait_send()
    swap1.wait_send()
    swap2.wait_send()
    gather_states.drain()
    return_states.drain()
    ring_a.drain()
    ring_z.drain()
    ring_o.drain()


def per_device(
    tokens, w_in, conv_weight, conv_bias, dt_bias, decay_rate, skip_gain, norm_gain, w_out
):
    chips, n_dp = lax.axis_size("seq") // 2, lax.axis_size("dp")
    rows = HALO + BLOCK
    tile_rows = 2 * N // chips
    dma = pltpu.SemaphoreType.DMA
    vmem = pl.BlockSpec(memory_space=pltpu.VMEM)
    return pl.pallas_call(
        functools.partial(mixer_kernel, chips, n_dp),
        out_shape=jax.ShapeDtypeStruct((BLOCK, 2 * N), BF),
        in_specs=[pl.BlockSpec(memory_space=pl.ANY)] + [vmem] * 8,
        out_specs=vmem,
        scratch_shapes=[
            pltpu.VMEM((rows, tokens.shape[1]), BF),
            pltpu.VMEM((chips, 2, AROWS, N), BF),
            pltpu.VMEM((chips, 2, ZC, N), BF),
            pltpu.VMEM((chips, 2, ZC, N), BF),
            pltpu.VMEM((rows, ZC + XG), F32),
            pltpu.VMEM((rows, 16), F32),
            pltpu.VMEM((rows, XG), F32),
            pltpu.VMEM((N + 16, 2 * N), BF),
            pltpu.VMEM((N + 16, 2 * N), BF),
            pltpu.VMEM((chips, tile_rows + 16, N), BF),
            pltpu.VMEM((chips, tile_rows + 16, N), BF),
            pltpu.VMEM((chips, tile_rows, N), BF),
            pltpu.VMEM((chips, tile_rows, N), BF),
            pltpu.VMEM((N, 2 * N), BF),
            pltpu.VMEM((2, N, 2 * N), BF),
            pltpu.VMEM((BLOCK, ZC), BF),
            pltpu.VMEM((chips, BLOCK, 2 * N), BF),
            pltpu.VMEM((n_dp, BLOCK, 2 * N), BF),
            dma, dma, dma, dma, dma, dma, dma,
            dma((chips,)), dma((chips,)), dma((chips,)), dma((chips,)), dma((chips,)), dma((n_dp,)),
            *ring_sems(chips),
            *ring_sems(chips),
            *ring_sems(chips),
        ],
        compiler_params=pltpu.CompilerParams(
            collective_id=0, has_side_effects=True, vmem_limit_bytes=VMEM_LIMIT
        ),
    )(
        tokens, w_in, conv_weight, conv_bias[None], dt_bias[None], decay_rate[None], skip_gain[None],
        norm_gain[None], w_out,
    )


def solution(mesh):
    placed = (
        P("seq", None),
        P("seq", "dp"),
        P(None, "dp"),
        P("dp"),
        P("dp"),
        P("dp"),
        P("dp"),
        P("dp"),
        P("dp", "seq"),
    )
    return jax.shard_map(
        per_device, mesh=mesh, in_specs=placed, out_specs=P("seq", "dp"), check_vma=False
    )
```

time: 503 us -> 138 us (0.27)
  waiting for transfers between devices: 215 us -> 0 us
  starting transfers between devices: 145 us -> 0 us
  Pallas kernels: 108 us -> 132 us
  between operations: 13.6 us -> 0.01 us
  other arithmetic: 8.17 us -> 0 us
  matrix products: 6.77 us -> 0 us
    ppermute x31 -> x0, starting transfers between devices: 145 us -> none  [from_behind(): return lax.ppermute(block, axis, route)]
    reduce_scatter x1 -> x0, waiting for transfers between devices: 112 us -> none  [per_device(): lax.psum_scatter(terms.astype(jnp.bfloat16), 'dp', scatter_dimension=1, t...]
    ppermute x31 -> x0, waiting for transfers between devices: 102 us -> none  [from_behind(): return lax.ppermute(block, axis, route)]
    pallas_call x1, Pallas kernels: 108 us -> 132 us  [per_device(): pl.pallas_call(functools.partial(mixer_kernel, chips, n_dp), out_shape=ja...]
    dot_general x5 -> x0, matrix products: 6.77 us -> none  [the longest x1 3.94 us: per_device(): jnp.dot(normed, lax.all_gather(w_out, 'seq', axis=1, tiled=True), preferr...]
    convert_element_type x63 -> x0, other arithmetic: 5.21 us -> none  [the longest x31 4.05 us: relay(): outgoing.astype(jnp.bfloat16)]
  transfers between devices with their start and end apart: 33 -> 0, of which waited for: 32 -> 0; matrix products, arithmetic and copies ran while one was open for 3% -> 0% of each run, Pallas kernels for 22% -> 0%
where the time goes in v2:
time: 138 us; the launch traced here: 137 us
  Pallas kernels  132 us (96%)
  local copies, waits for them, and re-layouts  4.61 us (3%)
    pallas_call x1, Pallas kernels, per_device(): pl.pallas_call(functools.partial(mixer_kernel, chips, n_dp), out_shape=ja...  132 us
    unnamed x4, local copies, waits for them, and re-layouts  4.03 us

profile of v2, /device:TPU:1, one launch (start us, length us, event | category | flops | bytes accessed | tf_op | source)
XLA Modules:
  0.0 136.6 jit_solution(1520350127716038022)
XLA Ops:
  0.0 0.0 copy-start
  0.0 0.7 copy-done
  0.7 0.6 broadcast_in_dim.15.cbias_ref
  1.3 1.9 %copy.10.win_ref = bf16[128,1288]{1,0:T(8,128)(2,1)} copy(bf16[128,1288]{0,1:T(8,128)(2,1)} %param.10) | data formatting | bytes 659456 | tf_op args[1]
  3.1 131.9 %shard_map.91 = bf16[128,256]{1,0:T(8,128)(2,1)} custom-call(bf16[128,4096]{1,0:T(8,128)(2,1)} %tok_hbm.1, bf16[128,1288]{1,0:T(8,128)(2,1)} %copy.10.win_ref, f32[4,768]{1,0:T(4,128)} %taps_ref.1, f32[1,768]{1,0:T(1,128)} %broadcast_in_dim.15.cbias_ref, f32[1,8]{1,0:T(1,128)} %bitcast.5, f32[1,8]{1,0:T(1,128)} %bitcast.6, f32[1,8]{1,0:T(1,128)} %bitcast.7, ...), custom_call_target="tpu_custom_call" | custom-call | tf_op jit(solution)/shard_map/pallas_call | solution.py:534
  135.1 1.5 %copy.12 = bf16[128,256]{1,0:T(8,128)(2,1)} copy(bf16[128,256]{1,0:T(8,128)(2,1)} %shard_map.91) | data formatting | bytes 131072
Async XLA Ops:
  0.0 0.7 copy-start

commit v3 on v2

v3 whole, which is shorter than its diff:
```python
import functools
import math

import jax
import jax.numpy as jnp
from jax import lax
from jax.experimental import pallas as pl
from jax.experimental.pallas import tpu as pltpu
from jax.sharding import PartitionSpec as P

P_SIZE = 64
N = 128
KCONV = 4
BLOCK = 128
HALF = 64
HG = 8
XG = 768
CG = 1288
ZC = 512
HALO = 8
AROWS = 16 + XG
XT = ZC // N
BF = jnp.bfloat16
F32 = jnp.float32
MESH = pl.DeviceIdType.MESH
HIGHEST = lax.Precision.HIGHEST
VMEM_LIMIT = 56 * 1024 * 1024

A_PARTS = ((0, 208), (208, 192), (400, 192), (592, 192))
W_PARTS = ((0, 128), (128, 128), (256, 128), (384, 128))

STAGES = (1, 2, 3, 5)


class Ring:
    def __init__(self, buf, parts, chips, core, right, left, sib, sems):
        self.buf, self.parts, self.chips, self.core = buf, parts, chips, core
        self.right, self.left, self.sib = right, left, sib
        self.recv, self.sent, self.srecv, self.ssent = sems
        self.half = chips // 2
        self.n = len(parts)

    def far(self, h, going_right):
        return (h < self.n // 2) == going_right

    def _hop(self, q, to, step, h, going_right):
        lo, size = self.parts[h]
        way = 0 if going_right else 1
        if isinstance(step, int):
            last = 2 if step == self.half - 1 else 0
        else:
            last = jnp.where(step == self.half - 1, 2, 0)
        return pltpu.make_async_remote_copy(
            src_ref=self.buf.at[q, self.core, pl.ds(lo, size)],
            dst_ref=self.buf.at[to, self.core, pl.ds(lo, size)],
            send_sem=self.sent.at[way + last],
            recv_sem=self.recv.at[step, h],
            device_id=self.right if going_right else self.left,
            device_id_type=MESH,
        )

    def _share(self, q, step):
        return pltpu.make_async_remote_copy(
            src_ref=self.buf.at[q, self.core],
            dst_ref=self.buf.at[q, self.core],
            send_sem=self.ssent,
            recv_sem=self.srecv.at[step],
            device_id=self.sib,
            device_id_type=MESH,
        )

    def _share_part(self, q, step, h):
        lo, size = self.parts[h]
        place = self.buf.at[q, self.core, pl.ds(lo, size)]
        return self._taken(place, self.ssent, self.srecv.at[step])

    def _taken(self, ref, send_sem, recv_sem):
        return pltpu.make_async_remote_copy(
            src_ref=ref, dst_ref=ref, send_sem=send_sem, recv_sem=recv_sem,
            device_id=self.sib, device_id_type=MESH,
        )

    def begin(self):
        for h in range(self.n):
            self._hop(0, 1, 0, h, True).start()
            self._hop(0, self.chips - 1, 0, h, False).start()
        self._share(0, 0).start()

    def step(self, k):
        z = self.chips
        final = isinstance(k, int) and k == self.half
        for h in range(self.n):
            lo, size = self.parts[h]
            places = self.buf.at[pl.ds(0, 1 if final else 2), self.core, pl.ds(lo, size)]
            self._taken(places, self.ssent, self.recv.at[k - 1, h]).wait_recv()
            if final:
                self._share_part(k, k, h).start()
                continue
            right = self._hop(k, k + 1, k, h, True)
            left = self._hop(z - k, z - k - 1, k, h, False)
            far, near = (right, left) if self.far(h, True) else (left, right)
            far.start()
            pl.when(k < self.half - 1)(near.start)
        if not final:
            self._share(k, k).start()
            self._share(z - k, k).start()

    def shared(self, k):
        both = 1 if isinstance(k, int) and k in (0, self.half) else 2
        places = self.buf.at[pl.ds(0, both), self.core]
        self._taken(places, self.ssent, self.srecv.at[k]).wait_recv()

    def drain(self):
        for way in range(2):
            blocks = self.buf.at[pl.ds(0, self.half - 1), self.core]
            self._taken(blocks, self.sent.at[way], self.srecv.at[0]).wait_send()
            hs = [h for h in range(self.n) if self.far(h, way == 0)]
            lo, size = self.parts[hs[0]][0], sum(self.parts[h][1] for h in hs)
            rows = self.buf.at[0, self.core, pl.ds(lo, size)]
            self._taken(rows, self.sent.at[2 + way], self.srecv.at[0]).wait_send()
        self._taken(self.buf.at[:, self.core], self.ssent, self.srecv.at[0]).wait_send()


def ring_sems(chips, parts):
    dma = pltpu.SemaphoreType.DMA
    return [dma((chips // 2, len(parts))), dma((4,)), dma((chips // 2 + 1,)), dma]


class Exchange:
    def __init__(self, out, inn, chips, z, peer, sent, recv):
        self.out, self.inn, self.chips, self.z, self.peer = out, inn, chips, z, peer
        self.sent, self.recv = sent, recv
        half = chips // 2
        self.order = [half] + [k for j in range(1, half) for k in (half - j, half + j)]

    def _copy(self, src, dst, device):
        return pltpu.make_async_remote_copy(
            src_ref=src, dst_ref=dst, send_sem=self.sent, recv_sem=self.recv,
            device_id=device, device_id_type=MESH,
        )

    def begin(self):
        for k in self.order:
            o = lax.rem(self.z + k, self.chips)
            self._copy(self.out.at[o], self.inn.at[self.z], self.peer(o)).start()
        self.inn[self.z] = self.out[self.z]

    def _all(self):
        others = pl.ds(0, self.chips - 1)
        return self._copy(self.out.at[others], self.inn.at[others], self.peer(self.z))

    def arrive(self):
        self._all().wait_recv()

    def drain(self):
        self._all().wait_send()


def silu(v):
    return v / (1.0 + jnp.exp(-v))


def two_parts(row):
    shape = (16, row.shape[1])
    high = row.astype(BF).astype(F32)
    low = row - high
    at = lax.broadcasted_iota(jnp.int32, shape, 0)
    high, low = jnp.broadcast_to(high, shape), jnp.broadcast_to(low, shape)
    return jnp.where(at == 0, high, jnp.where(at == 1, low, 0.0)).astype(BF)


def one_row(tile):
    tile = tile.astype(F32)
    return tile[0:1] + tile[1:2]


def head_lanes(values, j):
    shape = (values.shape[0], N)
    lane = lax.broadcasted_iota(jnp.int32, shape, 1)
    first = jnp.broadcast_to(values[:, 2 * j : 2 * j + 1], shape)
    second = jnp.broadcast_to(values[:, 2 * j + 1 : 2 * j + 2], shape)
    return jnp.where(lane < P_SIZE, first, second)


def mixer_kernel(
    chips, n_dp,
    tok_hbm, win_hbm, taps_hbm, cbias_hbm, dtb_hbm, rate_hbm, skip_hbm, gain_hbm, wout_hbm,
    out_ref,
    taps_ref, cbias_ref, dtb_ref, rate_ref, skip_ref, gain_ref, win_ref,
    tokx, buf_a, buf_z, buf_o, acc, acc_dt, xf, x1_out, x1_in, st_out, st_in, fade_out, fade_in, kept_ref, kept_fade_ref, c_ref, cum_ref, y_ref, hin_out, hin_in,
    x2_out, hfull, normed, t_out, r_in, p_out, p_in,
    local_sem, halo_send, halo_recv, x1_send, x1_recv, x2_send, x2_recv,
    e1_send, e1_recv, f1_send, f1_recv, e2_send, e2_recv, rs_send, rs_recv, *sems,
):
    d, s = lax.axis_index("dp"), lax.axis_index("seq")
    n_seq = 2 * chips
    half = chips // 2
    core, z = lax.rem(s, 2), s // 2
    right = (d, lax.rem(s + 2, n_seq))
    left = (d, lax.rem(s + n_seq - 2, n_seq))
    sib = (d, s + 1 - 2 * core)
    nxt = (d, lax.rem(s + 1, n_seq))
    odd = (d, lax.rem(s + n_seq - 1 + 2 * core, n_seq))
    tile_rows = 2 * N // chips
    side = math.isqrt(n_dp)
    y_at, x_at = d // side, lax.rem(d, side)

    sources = [
        (win_hbm, win_ref), (wout_hbm, buf_o.at[0, core]), (tok_hbm, tokx),
        (taps_hbm, taps_ref), (cbias_hbm, cbias_ref.at[0]),
        (dtb_hbm, dtb_ref), (rate_hbm, rate_ref), (skip_hbm, skip_ref), (gain_hbm, gain_ref),
    ]
    n_first = 2
    local = [
        pltpu.make_async_copy(here, there, local_sem.at[i]) for i, (here, there) in enumerate(sources)
    ]
    first, own, later = local[:n_first], local[n_first], local[n_first + 1 :]
    for copy in local:
        copy.start()

    barrier = pltpu.get_barrier_semaphore()

    def greet(device):
        pl.semaphore_signal(barrier, inc=1, device_id=device, device_id_type=MESH)

    greet(right)
    greet(left)

    @pl.loop(1, side)
    def _(k):
        greet((y_at * side + lax.rem(x_at + k, side), s))
        greet((lax.rem(y_at + k, side) * side + x_at, s))

    greet(sib)
    greet(odd)

    acc[...] = jnp.zeros_like(acc)
    acc_dt[...] = jnp.zeros_like(acc_dt)
    for copy in first:
        copy.wait()
    buf_a[0, core, 0:XG] = win_ref[ZC : ZC + XG]
    last_rows = win_ref[ZC + XG : CG].astype(F32)
    buf_a[0, core, XG:AROWS] = jnp.concatenate([last_rows, jnp.zeros((16 - HG, N), F32)], axis=0).astype(BF)
    buf_z[0, core] = win_ref[0:ZC]
    pl.semaphore_wait(barrier, 2 * side + 2)

    ring_a = Ring(buf_a, A_PARTS, chips, core, right, left, sib, sems[0:4])
    ring_z = Ring(buf_z, W_PARTS, chips, core, right, left, sib, sems[4:8])
    ring_o = Ring(buf_o, W_PARTS, chips, core, right, left, sib, sems[8:12])
    ring_a.begin()
    for copy in later:
        copy.wait()
    own.wait()

    def columns_of(q):
        owner = lax.rem(z - q + chips, chips)
        return pl.ds(pl.multiple_of(owner * 2 * N, 2 * N), 2 * N)

    turned = (((1,), (1,)), ((), ()))

    def both_cores(buf, q, row, size):
        return jnp.concatenate([buf[q, 0, row : row + size], buf[q, 1, row : row + size]], axis=1)

    def use_a(q):
        t = tokx[:, columns_of(q)]
        w = both_cores(buf_a, q, XG, 16)
        acc_dt[...] += lax.dot_general(t, w, turned, preferred_element_type=F32)
        for i in range(XG // (2 * N)):
            w = both_cores(buf_a, q, i * 2 * N, 2 * N)
            acc[:, pl.ds(ZC + i * 2 * N, 2 * N)] += lax.dot_general(t, w, turned, preferred_element_type=F32)

    def use_z(q):
        t = tokx[:, columns_of(q)]
        for i in range(ZC // (2 * N)):
            w = both_cores(buf_z, q, i * 2 * N, 2 * N)
            acc[:, pl.ds(i * 2 * N, 2 * N)] += lax.dot_general(t, w, turned, preferred_element_type=F32)

    def use_both(ring, use, k):
        ring.shared(k)
        use(k)
        if not (isinstance(k, int) and k in (0, half)):
            use(chips - k)

    use_both(ring_a, use_a, 0)

    @pl.loop(1, half)
    def _(k):
        ring_a.step(k)

        @pl.when(k > 1)
        def _():
            use_both(ring_a, use_a, k - 1)

    ring_z.begin()
    ring_o.begin()
    use_both(ring_a, use_a, half - 1)
    ring_a.step(half)
    use_both(ring_z, use_z, 0)
    use_both(ring_a, use_a, half)

    halo = pltpu.make_async_remote_copy(
        src_ref=acc.at[pl.ds(BLOCK - HALO, HALO), pl.ds(ZC, XG)],
        dst_ref=xf.at[pl.ds(0, HALO)],
        send_sem=halo_send,
        recv_sem=halo_recv,
        device_id=nxt,
        device_id_type=MESH,
    )
    halo.start()
    xf[HALO:, :] = acc[:, ZC:].astype(BF).astype(F32)
    halo.wait_recv()

    keep = jnp.where(s == 0, 0.0, 1.0)
    act = []
    for t in range(XG // N):
        cols = slice(t * N, (t + 1) * N)
        xf[0:HALO, cols] = xf[0:HALO, cols].astype(BF).astype(F32) * keep
        conv = jnp.broadcast_to(cbias_ref[0:1, cols], (BLOCK, N))
        for k in range(KCONV):
            start = HALO - KCONV + 1 + k
            conv = conv + taps_ref[k : k + 1, cols] * xf[start : start + BLOCK, cols]
        act.append(silu(conv))
    xs, bmat, cmat = act[:XT], act[XT], act[XT + 1]

    draw = acc_dt[:, 0:HG].astype(BF).astype(F32) + dtb_ref[0:1, :]
    dt = jnp.maximum(draw, 0.0) + jnp.log1p(jnp.exp(-jnp.abs(draw)))
    rows = lax.broadcasted_iota(jnp.int32, (BLOCK, BLOCK), 0)
    cols = lax.broadcasted_iota(jnp.int32, (BLOCK, BLOCK), 1)
    causal = rows >= cols
    cum = jnp.dot(
        causal.astype(F32), -dt * rate_ref[0:1, :], preferred_element_type=F32, precision=HIGHEST
    )
    cum_rows = jnp.concatenate([cum, jnp.zeros((BLOCK, N - HG), F32)], axis=1).T
    end = cum[BLOCK - 1 : BLOCK]
    tail = jnp.exp(end - cum)
    whole = jnp.exp(end)


    b_turned = bmat.T.astype(BF)
    dosed = [xs[j] * head_lanes(dt, j) for j in range(XT)]
    states = [
        jnp.dot(b_turned, (dosed[j] * head_lanes(tail, j)).astype(BF), preferred_element_type=F32)
        for j in range(XT)
    ]
    fades = [head_lanes(whole, j) for j in range(XT)]
    pair = XT // 2
    first_core = core == 0

    def joined(parts):
        return jnp.concatenate(parts, axis=1)

    low_state, high_state = joined(states[:pair]), joined(states[pair:])
    low_fade, high_fade = joined(fades[:pair]), joined(fades[pair:])
    kept_ref[...] = jnp.where(first_core, low_state, high_state)
    kept_fade_ref[...] = jnp.where(first_core, low_fade, high_fade)
    c_ref[...] = cmat.astype(BF)
    cum_ref[...] = cum
    x1_out[0:N] = jnp.where(first_core, high_state, low_state).astype(BF)
    x1_out[N : N + 16] = two_parts(jnp.where(first_core, high_fade, low_fade))
    swap1 = pltpu.make_async_remote_copy(
        src_ref=x1_out, dst_ref=x1_in, send_sem=x1_send, recv_sem=x1_recv,
        device_id=sib, device_id_type=MESH,
    )
    swap1.start()


    scores = lax.dot_general(
        cmat.astype(BF), bmat.astype(BF), (((1,), (1,)), ((), ())), preferred_element_type=F32
    )
    lane = lax.broadcasted_iota(jnp.int32, (BLOCK, N), 1)

    def inner(j):
        mix = []
        for h in (2 * j, 2 * j + 1):
            gap = jnp.where(causal, cum[:, h : h + 1] - cum_rows[h : h + 1, :], -1e30)
            mix.append((jnp.exp(gap) * scores).astype(BF))
        low = jnp.where(lane < P_SIZE, dosed[j], 0.0).astype(BF)
        high = jnp.where(lane < P_SIZE, 0.0, dosed[j]).astype(BF)
        y = jnp.dot(
            jnp.concatenate(mix, axis=1), jnp.concatenate([low, high], axis=0),
            preferred_element_type=F32,
        )
        return y + head_lanes(skip_ref[0:1, :], j) * xs[j]

    for j in range(XT):
        y_ref[:, j * N : (j + 1) * N] = inner(j)

    def peer(o):
        return (d, 2 * o + core)

    gather_fades = Exchange(fade_out, fade_in, chips, z, peer, f1_send, f1_recv)
    gather_states = Exchange(st_out, st_in, chips, z, peer, e1_send, e1_recv)
    return_states = Exchange(hin_out, hin_in, chips, z, peer, e2_send, e2_recv)
    swap2 = pltpu.make_async_remote_copy(
        src_ref=x2_out, dst_ref=hfull.at[core], send_sem=x2_send, recv_sem=x2_recv,
        device_id=sib, device_id_type=MESH,
    )

    def pair_states():
        swap1.wait_recv()
        kept, kept_fade = kept_ref[...], kept_fade_ref[...]
        other = x1_in[0:N].astype(F32)
        other_fade = one_row(x1_in[N : N + 16])
        state0 = jnp.where(first_core, kept, other)
        state1 = jnp.where(first_core, other, kept)
        fade0 = jnp.where(first_core, kept_fade, other_fade)
        fade1 = jnp.where(first_core, other_fade, kept_fade)
        kept_ref[...] = state0
        kept_fade_ref[...] = fade0
        chip_state = (state0 * fade1 + state1).astype(BF)
        chip_fade = fade0 * fade1
        for o in range(chips):
            i, j = o % half, o // half
            st_out[o] = chip_state[i * tile_rows : (i + 1) * tile_rows, j * N : (j + 1) * N]
            fade_out[o] = chip_fade[:, j * N : (j + 1) * N]
        gather_fades.begin()
        gather_states.begin()

    def scan_chips():
        gather_fades.arrive()
        gather_states.arrive()
        carry = jnp.zeros((tile_rows, N), F32)
        for q in range(chips):
            hin_out[q] = carry.astype(BF)
            carry = carry * fade_in[q] + st_in[q].astype(F32)
        return_states.begin()

    def enter():
        return_states.arrive()
        entry = joined([hin_in[j * half : (j + 1) * half].reshape(N, N) for j in range(pair)]).astype(F32)
        middle = entry * kept_fade_ref[...] + kept_ref[...]
        x2_out[...] = jnp.where(first_core, middle, entry).astype(BF)
        swap2.start()
        hfull[core] = jnp.where(first_core, entry, middle).astype(BF)

    def outer():
        swap2.wait_recv()
        grown = jnp.exp(cum_ref[...])
        for j in range(XT):
            h_in = hfull[j // pair, :, (j % pair) * N : (j % pair + 1) * N]
            y_ref[:, j * N : (j + 1) * N] += head_lanes(grown, j) * jnp.dot(
                c_ref[...], h_in, preferred_element_type=F32
            )

    stages = (pair_states, scan_chips, enter, outer)
    places = STAGES if half >= 8 else (1, 1, 1, 1)

    @pl.loop(1, half)
    def _(k):
        ring_z.step(k)
        ring_o.step(k)

        @pl.when(k > 1)
        def _():
            use_both(ring_z, use_z, k - 1)

        for place, stage in zip(places, stages):
            pl.when(k == place)(stage)

    use_both(ring_z, use_z, half - 1)
    ring_z.step(half)
    ring_o.step(half)
    use_both(ring_z, use_z, half)

    gated = []
    square = jnp.zeros((BLOCK, 1), F32)
    for j in range(XT):
        g = y_ref[:, j * N : (j + 1) * N] * silu(acc[:, j * N : (j + 1) * N].astype(BF).astype(F32))
        square = square + jnp.sum(g * g, axis=1, keepdims=True)
        gated.append(g)
    scale = lax.rsqrt(square / ZC + 1e-05)
    for j in range(XT):
        normed[:, j * N : (j + 1) * N] = (gated[j] * scale * gain_ref[0:1, j * N : (j + 1) * N]).astype(BF)

    ring_o.shared(0)
    ring_o.shared(half)

    @pl.loop(1, half)
    def _(k):
        ring_o.shared(k)

    def hand(src, dst, along, place, send_sem, recv_sem):
        there = (y_at * side + place, s) if along == 0 else (place * side + x_at, s)
        return pltpu.make_async_remote_copy(
            src_ref=src, dst_ref=dst, send_sem=send_sem, recv_sem=recv_sem,
            device_id=there, device_id_type=MESH,
        )

    at = (x_at, y_at)

    @pl.loop(0, n_dp)
    def _(i):
        yo, xo = lax.rem(y_at + 1 + i // side, side), lax.rem(x_at + 1 + i, side)
        q = lax.rem(z - (yo * side + xo) + 2 * chips, chips)
        w = jnp.concatenate([buf_o[q, 0], buf_o[q, 1]], axis=1)
        value = jnp.dot(normed[...], w, preferred_element_type=F32).astype(BF)
        for h, (to, index) in enumerate(((xo, yo), (yo, xo))):
            part = value[h * HALF : (h + 1) * HALF]
            t_out[h, to, index] = part

            @pl.when(to != at[h])
            def _():
                hand(
                    t_out.at[h, to, index], r_in.at[h, at[h], index], h, to,
                    rs_send.at[h], rs_recv.at[h],
                ).start()

            @pl.when(to == at[h])
            def _():
                r_in[h, to, index] = part

    few = pl.ds(0, side - 1)
    for h in range(2):
        first_stage = hand(t_out.at[h, few], r_in.at[h, few], h, at[h], rs_send.at[h], rs_recv.at[h])
        first_stage.wait_recv()
        for j in range(1, side + 1):
            to = lax.rem(at[1 - h] + j, side)
            partial = jnp.zeros((HALF, 2 * N), F32)
            for e in range(side):
                partial = partial + r_in[h, e, to].astype(F32)
            p_out[h, to] = partial.astype(BF)
            if j < side:
                hand(
                    p_out.at[h, to], p_in.at[h, at[1 - h]], 1 - h, to, rs_send.at[2 + h], rs_recv.at[2 + h]
                ).start()
            else:
                p_in[h, to] = partial.astype(BF)
    for h in range(2):
        second_stage = hand(
            p_out.at[h, few], p_in.at[h, few], h, at[h], rs_send.at[2 + h], rs_recv.at[2 + h]
        )
        second_stage.wait_recv()
        total = jnp.zeros((HALF, 2 * N), F32)
        for e in range(side):
            total = total + p_in[h, e].astype(F32)
        out_ref[h * HALF : (h + 1) * HALF] = total.astype(BF)
        second_stage.wait_send()
        hand(t_out.at[h, few], r_in.at[h, few], h, at[h], rs_send.at[h], rs_recv.at[h]).wait_send()
    halo.wait_send()
    swap1.wait_send()
    swap2.wait_send()
    gather_fades.drain()
    gather_states.drain()
    return_states.drain()
    ring_a.drain()
    ring_z.drain()
    ring_o.drain()


def per_device(
    tokens, w_in, conv_weight, conv_bias, dt_bias, decay_rate, skip_gain, norm_gain, w_out
):
    chips, n_dp = lax.axis_size("seq") // 2, lax.axis_size("dp")
    tile_rows = 2 * N // chips
    side = math.isqrt(n_dp)
    dma = pltpu.SemaphoreType.DMA
    vmem = pl.BlockSpec(memory_space=pltpu.VMEM)
    return pl.pallas_call(
        functools.partial(mixer_kernel, chips, n_dp),
        out_shape=jax.ShapeDtypeStruct((BLOCK, 2 * N), BF),
        in_specs=[pl.BlockSpec(memory_space=pl.ANY)] * 9,
        out_specs=vmem,
        scratch_shapes=[
            pltpu.VMEM((KCONV, XG), F32),
            pltpu.VMEM((1, XG), F32),
            pltpu.VMEM((1, HG), F32),
            pltpu.VMEM((1, HG), F32),
            pltpu.VMEM((1, HG), F32),
            pltpu.VMEM((1, ZC), F32),
            pltpu.VMEM((CG, N), BF),
            pltpu.VMEM(tokens.shape, BF),
            pltpu.VMEM((chips, 2, AROWS, N), BF),
            pltpu.VMEM((chips, 2, ZC, N), BF),
            pltpu.VMEM((chips, 2, ZC, N), BF),
            pltpu.VMEM((BLOCK, ZC + XG), F32),
            pltpu.VMEM((BLOCK, 16), F32),
            pltpu.VMEM((HALO + BLOCK, XG), F32),
            pltpu.VMEM((N + 16, 2 * N), BF),
            pltpu.VMEM((N + 16, 2 * N), BF),
            pltpu.VMEM((chips, tile_rows, N), BF),
            pltpu.VMEM((chips, tile_rows, N), BF),
            pltpu.VMEM((chips, 1, N), F32),
            pltpu.VMEM((chips, 1, N), F32),
            pltpu.VMEM((N, 2 * N), F32),
            pltpu.VMEM((1, 2 * N), F32),
            pltpu.VMEM((BLOCK, N), BF),
            pltpu.VMEM((BLOCK, HG), F32),
            pltpu.VMEM((BLOCK, ZC), F32),
            pltpu.VMEM((chips, tile_rows, N), BF),
            pltpu.VMEM((chips, tile_rows, N), BF),
            pltpu.VMEM((N, 2 * N), BF),
            pltpu.VMEM((2, N, 2 * N), BF),
            pltpu.VMEM((BLOCK, ZC), BF),
            pltpu.VMEM((2, side, side, HALF, 2 * N), BF),
            pltpu.VMEM((2, side, side, HALF, 2 * N), BF),
            pltpu.VMEM((2, side, HALF, 2 * N), BF),
            pltpu.VMEM((2, side, HALF, 2 * N), BF),
            dma((9,)), dma, dma, dma, dma, dma, dma,
            dma, dma, dma, dma, dma, dma, dma((4,)), dma((4,)),
            *ring_sems(chips, A_PARTS),
            *ring_sems(chips, W_PARTS),
            *ring_sems(chips, W_PARTS),
        ],
        compiler_params=pltpu.CompilerParams(
            collective_id=0, has_side_effects=True, vmem_limit_bytes=VMEM_LIMIT
        ),
    )(
        tokens, w_in.T, conv_weight, conv_bias, dt_bias[None], decay_rate[None], skip_gain[None],
        norm_gain[None], w_out,
    )


def solution(mesh):
    placed = (
        P("seq", None),
        P("seq", "dp"),
        P(None, "dp"),
        P("dp"),
        P("dp"),
        P("dp"),
        P("dp"),
        P("dp"),
        P("dp", "seq"),
    )
    return jax.shard_map(
        per_device, mesh=mesh, in_specs=placed, out_specs=P("seq", "dp"), check_vma=False
    )
```

time: 138 us -> 117 us (0.85); the launches traced: 137 us -> 117 us
  Pallas kernels: 132 us -> 116 us
  local copies, waits for them, and re-layouts: 4.61 us -> 1.47 us
    pallas_call x1, Pallas kernels: 132 us -> 116 us  [per_device(): pl.pallas_call(functools.partial(mixer_kernel, chips, n_dp), out_shape=ja...]
    unnamed x4 -> x1, local copies, waits for them, and re-layouts: 4.03 us -> 1.47 us
where the time goes in v3:
time: 117 us
  Pallas kernels  116 us (99%)
  local copies, waits for them, and re-layouts  1.47 us (1%)
    pallas_call x1, Pallas kernels, per_device(): pl.pallas_call(functools.partial(mixer_kernel, chips, n_dp), out_shape=ja...  116 us

profile of v3, /device:TPU:1, one launch (start us, length us, event | category | flops | bytes accessed | tf_op | source)
XLA Modules:
  0.0 117.2 jit_solution(16028387926852255846)
XLA Ops:
  0.0 115.7 %shard_map.91 = bf16[128,256]{1,0:T(8,128)(2,1)} custom-call(bf16[128,4096]{1,0:T(8,128)(2,1)} %tok_hbm.1, bf16[1288,128]{1,0:T(8,128)(2,1)} %bitcast.5, f32[4,768]{1,0:T(4,128)} %taps_hbm.1, f32[768]{0:T(1024)} %cbias_hbm.1, f32[1,8]{1,0:T(1,128)} %bitcast.7, f32[1,8]{1,0:T(1,128)} %bitcast.8, f32[1,8]{1,0:T(1,128)} %bitcast.9, f32[1,512]{1,0:T(1,128)} %bitcast.6, ...), custom_call_target="tpu_custom_call" | custom-call | tf_op jit(solution)/shard_map/pallas_call | solution.py:558
  115.8 1.5 %copy.11 = bf16[128,256]{1,0:T(8,128)(2,1)} copy(bf16[128,256]{1,0:T(8,128)(2,1)} %shard_map.91) | data formatting | bytes 131072

commit v4 on v3

--- a/solution.py
+++ b/solution.py
@@ -448,10 +448,10 @@
     @pl.loop(1, half)
     def _(k):
         ring_z.step(k)
-        ring_o.step(k)
 
         @pl.when(k > 1)
         def _():
+            ring_o.step(k - 1)
             use_both(ring_z, use_z, k - 1)
 
         for place, stage in zip(places, stages):
@@ -459,7 +459,7 @@
 
     use_both(ring_z, use_z, half - 1)
     ring_z.step(half)
-    ring_o.step(half)
+    ring_o.step(jnp.int32(half - 1))
     use_both(ring_z, use_z, half)
 
     gated = []
@@ -473,9 +473,8 @@
         normed[:, j * N : (j + 1) * N] = (gated[j] * scale * gain_ref[0:1, j * N : (j + 1) * N]).astype(BF)
 
     ring_o.shared(0)
-    ring_o.shared(half)
-
-    @pl.loop(1, half)
+
+    @pl.loop(1, half - 1)
     def _(k):
         ring_o.shared(k)
 
@@ -488,10 +487,7 @@
 
     at = (x_at, y_at)
 
-    @pl.loop(0, n_dp)
-    def _(i):
-        yo, xo = lax.rem(y_at + 1 + i // side, side), lax.rem(x_at + 1 + i, side)
-        q = lax.rem(z - (yo * side + xo) + 2 * chips, chips)
+    def term(yo, xo, q):
         w = jnp.concatenate([buf_o[q, 0], buf_o[q, 1]], axis=1)
         value = jnp.dot(normed[...], w, preferred_element_type=F32).astype(BF)
         for h, (to, index) in enumerate(((xo, yo), (yo, xo))):
@@ -508,6 +504,23 @@
             @pl.when(to == at[h])
             def _():
                 r_in[h, to, index] = part
+
+    def terms(of_last_steps):
+        @pl.loop(0, n_dp)
+        def _(i):
+            yo, xo = lax.rem(y_at + 1 + i // side, side), lax.rem(x_at + 1 + i, side)
+            q = lax.rem(z - (yo * side + xo) + 2 * chips, chips)
+            late = (q >= half - 1) & (q <= half + 1)
+
+            @pl.when(late if of_last_steps else ~late)
+            def _():
+                term(yo, xo, q)
+
+    terms(False)
+    ring_o.step(half)
+    ring_o.shared(half - 1)
+    ring_o.shared(half)
+    terms(True)
 
     few = pl.ds(0, side - 1)
     for h in range(2):

time: 117 us -> 116 us (level)
  Pallas kernels: 116 us -> 114 us
    pallas_call x1, Pallas kernels: 116 us -> 114 us  [per_device(): pl.pallas_call(functools.partial(mixer_kernel, chips, n_dp), out_shape=ja...]
where the time goes in v4:
time: 116 us
  Pallas kernels  114 us (98%)
  local copies, waits for them, and re-layouts  1.47 us (1%)
    pallas_call x1, Pallas kernels, per_device(): pl.pallas_call(functools.partial(mixer_kernel, chips, n_dp), out_shape=ja...  114 us

profile of v4, /device:TPU:1, one launch (start us, length us, event | category | flops | bytes accessed | tf_op | source)
XLA Modules:
  0.0 115.9 jit_solution(11316733047779813727)
XLA Ops:
  0.0 114.4 %shard_map.91 = bf16[128,256]{1,0:T(8,128)(2,1)} custom-call(bf16[128,4096]{1,0:T(8,128)(2,1)} %tok_hbm.1, bf16[1288,128]{1,0:T(8,128)(2,1)} %bitcast.5, f32[4,768]{1,0:T(4,128)} %taps_hbm.1, f32[768]{0:T(1024)} %cbias_hbm.1, f32[1,8]{1,0:T(1,128)} %bitcast.7, f32[1,8]{1,0:T(1,128)} %bitcast.8, f32[1,8]{1,0:T(1,128)} %bitcast.9, f32[1,512]{1,0:T(1,128)} %bitcast.6, ...), custom_call_target="tpu_custom_call" | custom-call | tf_op jit(solution)/shard_map/pallas_call | solution.py:571
  114.4 1.5 %copy.11 = bf16[128,256]{1,0:T(8,128)(2,1)} copy(bf16[128,256]{1,0:T(8,128)(2,1)} %shard_map.91) | data formatting | bytes 131072

commit v5 on v4

--- a/solution.py
+++ b/solution.py
@@ -26,7 +26,7 @@
 HIGHEST = lax.Precision.HIGHEST
 VMEM_LIMIT = 56 * 1024 * 1024
 
-A_PARTS = ((0, 208), (208, 192), (400, 192), (592, 192))
+A_PARTS = ((0, 112), (112, 96), (208, 96), (304, 96), (400, 96), (496, 96), (592, 96), (688, 96))
 W_PARTS = ((0, 128), (128, 128), (256, 128), (384, 128))
 
 STAGES = (1, 2, 3, 5)
@@ -184,9 +184,9 @@
 
 def mixer_kernel(
     chips, n_dp,
-    tok_hbm, win_hbm, taps_hbm, cbias_hbm, dtb_hbm, rate_hbm, skip_hbm, gain_hbm, wout_hbm,
+    tok_hbm, win_ref, taps_hbm, cbias_hbm, dtb_hbm, rate_hbm, skip_hbm, gain_hbm, wout_hbm,
     out_ref,
-    taps_ref, cbias_ref, dtb_ref, rate_ref, skip_ref, gain_ref, win_ref,
+    taps_ref, cbias_ref, dtb_ref, rate_ref, skip_ref, gain_ref,
     tokx, buf_a, buf_z, buf_o, acc, acc_dt, xf, x1_out, x1_in, st_out, st_in, fade_out, fade_in, kept_ref, kept_fade_ref, c_ref, cum_ref, y_ref, hin_out, hin_in,
     x2_out, hfull, normed, t_out, r_in, p_out, p_in,
     local_sem, halo_send, halo_recv, x1_send, x1_recv, x2_send, x2_recv,
@@ -206,11 +206,11 @@
     y_at, x_at = d // side, lax.rem(d, side)
 
     sources = [
-        (win_hbm, win_ref), (wout_hbm, buf_o.at[0, core]), (tok_hbm, tokx),
+        (wout_hbm, buf_o.at[0, core]), (tok_hbm, tokx),
         (taps_hbm, taps_ref), (cbias_hbm, cbias_ref.at[0]),
         (dtb_hbm, dtb_ref), (rate_hbm, rate_ref), (skip_hbm, skip_ref), (gain_hbm, gain_ref),
     ]
-    n_first = 2
+    n_first = 1
     local = [
         pltpu.make_async_copy(here, there, local_sem.at[i]) for i, (here, there) in enumerate(sources)
     ]
@@ -571,7 +571,7 @@
     return pl.pallas_call(
         functools.partial(mixer_kernel, chips, n_dp),
         out_shape=jax.ShapeDtypeStruct((BLOCK, 2 * N), BF),
-        in_specs=[pl.BlockSpec(memory_space=pl.ANY)] * 9,
+        in_specs=[pl.BlockSpec(memory_space=pl.ANY), vmem] + [pl.BlockSpec(memory_space=pl.ANY)] * 7,
         out_specs=vmem,
         scratch_shapes=[
             pltpu.VMEM((KCONV, XG), F32),
@@ -580,7 +580,6 @@
             pltpu.VMEM((1, HG), F32),
             pltpu.VMEM((1, HG), F32),
             pltpu.VMEM((1, ZC), F32),
-            pltpu.VMEM((CG, N), BF),
             pltpu.VMEM(tokens.shape, BF),
             pltpu.VMEM((chips, 2, AROWS, N), BF),
             pltpu.VMEM((chips, 2, ZC, N), BF),
@@ -608,7 +607,7 @@
             pltpu.VMEM((2, side, side, HALF, 2 * N), BF),
             pltpu.VMEM((2, side, HALF, 2 * N), BF),
             pltpu.VMEM((2, side, HALF, 2 * N), BF),
-            dma((9,)), dma, dma, dma, dma, dma, dma,
+            dma((8,)), dma, dma, dma, dma, dma, dma,
             dma, dma, dma, dma, dma, dma, dma((4,)), dma((4,)),
             *ring_sems(chips, A_PARTS),
             *ring_sems(chips, W_PARTS),

time: 116 us -> 116 us (level)
  no operation moved by 1% of the time
where the time goes in v5:
time: 116 us
  Pallas kernels  115 us (99%)
  local copies, waits for them, and re-layouts  1.47 us (1%)
    pallas_call x1, Pallas kernels, per_device(): pl.pallas_call(functools.partial(mixer_kernel, chips, n_dp), out_shape=ja...  115 us

profile of v5, /device:TPU:1, one launch (start us, length us, event | category | flops | bytes accessed | tf_op | source)
XLA Modules:
  0.0 116.0 jit_solution(1136907542130450572)
XLA Ops:
  0.0 114.5 %shard_map.91 = bf16[128,256]{1,0:T(8,128)(2,1)} custom-call(bf16[128,4096]{1,0:T(8,128)(2,1)} %tok_hbm.1, bf16[1288,128]{1,0:T(8,128)(2,1)} %bitcast.5, f32[4,768]{1,0:T(4,128)} %taps_hbm.1, f32[768]{0:T(1024)} %cbias_hbm.1, f32[1,8]{1,0:T(1,128)} %bitcast.7, f32[1,8]{1,0:T(1,128)} %bitcast.8, f32[1,8]{1,0:T(1,128)} %bitcast.9, f32[1,512]{1,0:T(1,128)} %bitcast.6, ...), custom_call_target="tpu_custom_call" | custom-call | tf_op jit(solution)/shard_map/pallas_call | solution.py:571
  114.6 1.5 %copy.11 = bf16[128,256]{1,0:T(8,128)(2,1)} copy(bf16[128,256]{1,0:T(8,128)(2,1)} %shard_map.91) | data formatting | bytes 131072
